TPU v7x, 128 devices: a whole 4x4x4 slice. The times are simulated.
128 devices in a mesh: gx: 4 (over z_hi, core), gy: 4 (over x), band: 8 (over z_lo, y).
Axes of the slice: x: 4, y: 4, z: 4 (z_hi: 2, z_lo: 2; z = z_hi * 2 + z_lo), core: 2. Of those that a mesh axis runs over, the one named last changes fastest.
Arguments:
- orbitals: float32 [64, 32, 32, 384], P('band', 'gx', 'gy'), may hold values from -6 to 6
- potential: float32 [32, 32, 384], P('gx', 'gy'), may hold values from -3 to 0
Outputs:
- filtered: float32 [64, 32, 32, 384], P('band', 'gx', 'gy')
- margin: float32 [64, 64], P('band')
- hamiltonian: float32 [64, 64], P('band')
All inputs are finite; a program needn't handle non-finite values.
Results may differ from a plain program's by a relative error of at most 0.000086.
Values sent between devices are 32-bit elements; how exact they have to be, the bound alone decides.
No kernel may reach another device: no remote copies, remote signals or barrier semaphores. Data moves between devices by JAX's collectives and lax.ppermute only.
A program may use at most 128 MiB of HBM per device.

v0:
```python
import jax
import jax.numpy as jnp
from jax import lax
from jax.sharding import PartitionSpec as P

DEGREE = 4


STENCIL_WEIGHTS = (
    -5369.0 / 1800.0,
    12.0 / 7.0,
    -15.0 / 56.0,
    10.0 / 189.0,
    -1.0 / 112.0,
    2.0 / 1925.0,
    -1.0 / 16632.0,
)
GRID_SPACING = 0.5
FILTER_CENTER = 24.0
FILTER_HALFWIDTH = 20.0
CONTRACT_CELLS = (((1,), (1,)), ((), ()))


def with_halo(array, sides, width):
    for axis, dim in sides:
        count, length = (lax.axis_size(axis), array.shape[dim])
        up = [(i, (i + 1) % count) for i in range(count)]
        down = [(j, i) for i, j in up]
        last = lax.slice_in_dim(array, length - width, length, axis=dim)
        leading = lax.slice_in_dim(array, 0, width, axis=dim)
        before = lax.ppermute(last, axis, up)
        after = lax.ppermute(leading, axis, down)
        array = jnp.concatenate([before, array, after], axis=dim)
    return array


def hamiltonian_apply(field, potential):
    rows_x = field.shape[1]
    rows_y = field.shape[2]
    padded = with_halo(field, (("gx", 1), ("gy", 2)), 6)
    laplacian = 3.0 * STENCIL_WEIGHTS[0] * field
    for reach in range(1, 7):
        along_x = (
            padded[:, 6 + reach : 6 + reach + rows_x, 6 : 6 + rows_y]
            + padded[:, 6 - reach : 6 - reach + rows_x, 6 : 6 + rows_y]
        )
        along_y = (
            padded[:, 6 : 6 + rows_x, 6 + reach : 6 + reach + rows_y]
            + padded[:, 6 : 6 + rows_x, 6 - reach : 6 - reach + rows_y]
        )
        along_z = jnp.roll(field, reach, 3) + jnp.roll(field, -reach, 3)
        laplacian = laplacian + STENCIL_WEIGHTS[reach] * (along_x + along_y + along_z)
    return -0.5 / (GRID_SPACING * GRID_SPACING) * laplacian + potential[None] * field


def inner_rows(left, right):
    return lax.dot_general(
        left,
        right,
        CONTRACT_CELLS,
        precision=lax.Precision.HIGHEST,
        preferred_element_type=jnp.float32,
    )


def per_device(orbitals, potential):
    previous = orbitals
    current = (hamiltonian_apply(orbitals, potential) - FILTER_CENTER * orbitals) / FILTER_HALFWIDTH
    for step in range(DEGREE - 1):
        following = (
            2.0
            * (hamiltonian_apply(current, potential) - FILTER_CENTER * current)
            / FILTER_HALFWIDTH
            - previous
        )
        previous, current = (current, following)
    applied = hamiltonian_apply(current, potential)
    orb_local = current.shape[0]
    flat = current.reshape(orb_local, -1)
    applied_flat = applied.reshape(orb_local, -1)
    scale = 1.0 / flat.shape[1]
    blocks, applied_blocks = (
        lax.all_to_all(flat, "band", split_axis=1, concat_axis=0, tiled=True),
        lax.all_to_all(applied_flat, "band", split_axis=1, concat_axis=0, tiled=True),
    )
    margin_full = inner_rows(blocks, blocks)
    hamilton_full = inner_rows(blocks, applied_blocks)
    margin_part, hamilton_part = (
        lax.psum_scatter(margin_full, "band", scatter_dimension=0, tiled=True),
        lax.psum_scatter(hamilton_full, "band", scatter_dimension=0, tiled=True),
    )
    margin_rows, hamilton_rows = lax.psum((margin_part, hamilton_part), ("gx", "gy"))
    return (current, margin_rows * scale, hamilton_rows * scale)


def solution(mesh):
    placed = (P("band", "gx", "gy", None), P("gx", "gy", None))
    return jax.shard_map(
        per_device,
        mesh=mesh,
        in_specs=placed,
        out_specs=(P("band", "gx", "gy", None), P("band", None), P("band", None)),
        check_vma=False,
    )
```

profile of v0, /device:TPU:2, one launch (start us, length us, event | category | flops | bytes accessed | tf_op | source)
XLA Modules:
  0.0 423.1 jit_solution(1708300006200423409)
XLA Ops:
  0.6 1.4 fusion.293
  2.5 3.4 collective-permute-start
  7.6 7.5 %collective-permute-done.1 = f32[8,6,8,384]{3,0,2,1:T(8,128)S(1)} collective-permute-done((f32[8,6,8,384]{3,0,2,1:T(8,128)S(1)}, f32[8,6,8,384]{3,0,2,1:T(8,128)S(1)}, u32[]{:S(2)}, u32[]{:S(2)}) %collective-permute-start.1) | collective-permute-done | bytes 589856 | tf_op jit(solution)/shard_map/ppermute | solution.py:31
  15.7 3.6 collective-permute-done
  20.3 1.6 collective-permute-start.3
  39.6 14.8 %collective-permute-done.2 = f32[8,20,6,384]{3,0,2,1:T(8,128)S(1)} collective-permute-done((f32[8,20,6,384]{3,0,2,1:T(8,128)S(1)}, f32[8,20,6,384]{3,0,2,1:T(8,128)S(1)}, u32[]{:S(2)}, u32[]{:S(2)}) %collective-permute-start.2) | collective-permute-done | bytes 1474592 | tf_op jit(solution)/shard_map/ppermute | solution.py:32
  54.4 1.4 collective-permute-done.3
  57.0 6.8 %broadcast_multiply_fusion = (f32[8,8,8,384]{3,0,2,1:T(8,128)S(1)}, f32[8,8,8,384]{3,0,2,1:T(8,128)S(1)}) fusion(f32[8,8,384]{2,1,0:T(8,128)S(1)} %copy-done.1, f32[8,8,8,6]{3,0,2,1:T(8,128)} %copy.70, f32[8,8,8,378]{3,0,2,1:T(8,128)} %copy.71, f32[8,8,8,378]{3,0,2,1:T(8,128)S(1)} %copy.68, f32[8,8,8,6]{3,0,2,1:T(8,128)} %copy.69, ...), kind=kLoop, calls=%fused_computation.407 | loop fusion | flops 14352384 | bytes 26247168 | tf_op jit(solution)/shard_map/div | solution.py:68
  66.5 1.5 collective-permute-start.4
  71.4 8.8 %collective-permute-done.4 = f32[8,6,8,384]{3,0,2,1:T(8,128)S(1)} collective-permute-done((f32[8,6,8,384]{3,0,2,1:T(8,128)S(1)}, f32[8,6,8,384]{3,0,2,1:T(8,128)S(1)}, u32[]{:S(2)}, u32[]{:S(2)}) %collective-permute-start.4) | collective-permute-done | bytes 589856 | tf_op jit(solution)/shard_map/ppermute | solution.py:32
  80.3 3.8 collective-permute-done.5
  84.5 3.0 collective-permute-start.6
  88.4 1.5 fusion.272
  89.9 1.4 fusion.274
  91.3 1.5 fusion.276
  92.7 1.4 fusion.278
  95.5 22.7 %collective-permute-done.6 = f32[8,20,6,384]{3,0,2,1:T(8,128)S(1)} collective-permute-done((f32[8,20,6,384]{3,0,2,1:T(8,128)S(1)}, f32[8,20,6,384]{3,0,2,1:T(8,128)S(1)}, u32[]{:S(2)}, u32[]{:S(2)}) %collective-permute-start.6) | collective-permute-done | bytes 1474592 | tf_op jit(solution)/shard_map/ppermute | solution.py:32
  120.6 3.7 pad_maximum_fusion
  124.3 6.9 %fusion.131 = f32[8,8,8,384]{3,0,2,1:T(8,128)S(1)} fusion(f32[8,8,8,384]{3,0,2,1:T(8,128)S(1)} %get-tuple-element.10, f32[8,6,8,384]{3,0,2,1:T(8,128)S(1)} %collective-permute-done.5, f32[8,6,8,384]{3,0,2,1:T(8,128)S(1)} %collective-permute-done.4, f32[8,20,14,384]{3,0,2,1:T(8,128)S(1)} %get-tuple-element.25, f32[8,20,14,384]{3,0,2,1:T(8,128)S(1)} %get-tuple-element.24, ...), kind=kLoop, calls=%fused_computation.243 | loop fusion | flops 14548992 | bytes 23298048 | tf_op jit(solution)/shard_map/sub | solution.py:71
  137.4 10.0 %collective-permute-done.8 = f32[8,6,8,384]{3,0,2,1:T(8,128)S(1)} collective-permute-done((f32[8,6,8,384]{3,0,2,1:T(8,128)S(1)}, f32[8,6,8,384]{3,0,2,1:T(8,128)S(1)}, u32[]{:S(2)}, u32[]{:S(2)}) %collective-permute-start.8) | collective-permute-done | bytes 589856 | tf_op jit(solution)/shard_map/ppermute | solution.py:32
  147.4 1.8 collective-permute-done.9
  149.6 2.0 collective-permute-start.10
  153.0 1.4 fusion.257
  154.4 1.4 fusion.259
  155.8 1.5 fusion.261
  158.6 1.4 fusion.265
  160.0 22.5 %collective-permute-done.10 = f32[8,20,6,384]{3,0,2,1:T(8,128)S(1)} collective-permute-done((f32[8,20,6,384]{3,0,2,1:T(8,128)S(1)}, f32[8,20,6,384]{3,0,2,1:T(8,128)S(1)}, u32[]{:S(2)}, u32[]{:S(2)}) %collective-permute-start.10) | collective-permute-done | bytes 1474592 | tf_op jit(solution)/shard_map/ppermute | solution.py:32
  184.5 3.7 pad_maximum_fusion.1
  188.3 6.5 %fusion.90 = f32[8,8,8,384]{3,0,2,1:T(8,128)S(1)} fusion(f32[8,8,8,384]{3,0,2,1:T(8,128)S(1)} %fusion.131, f32[8,6,8,384]{3,0,2,1:T(8,128)S(1)} %collective-permute-done.9, f32[8,6,8,384]{3,0,2,1:T(8,128)S(1)} %collective-permute-done.8, f32[8,20,14,384]{3,0,2,1:T(8,128)S(1)} %get-tuple-element.21, f32[8,20,14,384]{3,0,2,1:T(8,128)S(1)} %get-tuple-element.20, ...), kind=kLoop, calls=%fused_computation.202 | loop fusion | flops 14745600 | bytes 22511616 | tf_op jit(solution)/shard_map/sub | solution.py:71
  200.8 10.6 %collective-permute-done.12 = f32[8,6,8,384]{3,0,2,1:T(8,128)S(1)} collective-permute-done((f32[8,6,8,384]{3,0,2,1:T(8,128)S(1)}, f32[8,6,8,384]{3,0,2,1:T(8,128)S(1)}, u32[]{:S(2)}, u32[]{:S(2)}) %collective-permute-start.12) | collective-permute-done | bytes 589856 | tf_op jit(solution)/shard_map/ppermute | solution.py:32
  211.4 3.2 collective-permute-done.13
  215.0 2.4 collective-permute-start.14
  218.4 1.4 fusion.246
  219.9 1.4 fusion.248
  221.3 1.5 fusion.250
  222.7 1.4 fusion.252
  225.5 23.2 %collective-permute-done.14 = f32[8,20,6,384]{3,0,2,1:T(8,128)S(1)} collective-permute-done((f32[8,20,6,384]{3,0,2,1:T(8,128)S(1)}, f32[8,20,6,384]{3,0,2,1:T(8,128)S(1)}, u32[]{:S(2)}, u32[]{:S(2)}) %collective-permute-start.14) | collective-permute-done | bytes 1474592 | tf_op jit(solution)/shard_map/ppermute | solution.py:32
  251.2 3.7 pad_maximum_fusion.2
  254.9 7.1 %fusion.49 = f32[8,8,8,384]{3,0,2,1:T(8,128)} fusion(f32[8,8,8,384]{3,0,2,1:T(8,128)S(1)} %fusion.131, f32[8,8,8,384]{3,0,2,1:T(8,128)S(1)} %fusion.90, f32[8,6,8,384]{3,0,2,1:T(8,128)S(1)} %collective-permute-done.13, f32[8,6,8,384]{3,0,2,1:T(8,128)S(1)} %collective-permute-done.12, f32[8,20,14,384]{3,0,2,1:T(8,128)S(1)} %get-tuple-element.17, ...), kind=kLoop, calls=%fused_computation.161 | loop fusion | flops 14548992 | bytes 22511616 | tf_op jit(solution)/shard_map/sub | solution.py:71
  263.3 1.9 fusion.232
  265.2 1.9 fusion.234
  267.2 1.9 fusion.236
  269.6 1.9 fusion.238
  271.5 1.9 fusion.240
  273.4 1.7 fusion.231
  275.1 6.7 %collective-permute-done.16 = f32[8,6,8,384]{3,0,2,1:T(8,128)S(1)} collective-permute-done((f32[8,6,8,384]{3,0,2,1:T(8,128)S(1)}, f32[8,6,8,384]{3,0,2,1:T(8,128)S(1)}, u32[]{:S(2)}, u32[]{:S(2)}) %collective-permute-start.16) | collective-permute-done | bytes 589856 | tf_op jit(solution)/shard_map/ppermute | solution.py:32
  281.8 2.9 collective-permute-done.17
  286.0 1.8 fusion.226
  287.8 1.5 collective-permute-start.18
  289.8 1.9 fusion.242
  291.7 6.0 %all-to-all-start = ((f32[8,8,3072]{2,0,1:T(8,128)}), f32[8,8,3072]{2,0,1:T(8,128)S(1)}, u32[]{:S(2)}, u32[]{:S(2)}) async-start(f32[8,8,3072]{2,0,1:T(8,128)} %bitcast), calls=%async_computation | async-start | bytes 1572864 | tf_op jit(solution)/shard_map/all_to_all | solution.py:83
  297.7 2.5 fusion.233
  300.2 2.9 fusion.235
  303.1 2.8 fusion.237
  305.9 2.8 fusion.239
  308.7 2.8 fusion.241
  311.5 9.4 %collective-permute-done.18 = f32[8,20,6,384]{3,0,2,1:T(8,128)} collective-permute-done((f32[8,20,6,384]{3,0,2,1:T(8,128)}, f32[8,20,6,384]{3,0,2,1:T(8,128)}, u32[]{:S(2)}, u32[]{:S(2)}) %collective-permute-start.18) | collective-permute-done | bytes 1474592 | tf_op jit(solution)/shard_map/ppermute | solution.py:32
  322.0 2.8 pad_maximum_fusion.3
  324.8 8.8 %fusion.8 = f32[8,8,8,384]{3,0,2,1:T(8,128)} fusion(f32[8,8,8,384]{3,0,2,1:T(8,128)} %fusion.49, f32[8,6,8,384]{3,0,2,1:T(8,128)S(1)} %collective-permute-done.17, f32[8,6,8,384]{3,0,2,1:T(8,128)S(1)} %collective-permute-done.16, f32[8,20,14,384]{3,0,2,1:T(8,128)S(1)} %get-tuple-element.13, f32[8,20,14,384]{3,0,2,1:T(8,128)S(1)} %get-tuple-element.12, ...), kind=kLoop, calls=%fused_computation.120 | loop fusion | flops 13762560 | bytes 21725184 | tf_op jit(solution)/shard_map/add | solution.py:53
  333.7 7.3 %all-to-all-start.1 = ((f32[8,8,3072]{2,0,1:T(8,128)}), f32[8,8,3072]{2,0,1:T(8,128)S(1)}, u32[]{:S(2)}, u32[]{:S(2)}) async-start(f32[8,8,3072]{2,0,1:T(8,128)} %bitcast.4), calls=%async_computation.1 | async-start | bytes 1572864 | tf_op jit(solution)/shard_map/all_to_all | solution.py:84
  342.2 2.2 copy.40
  345.2 6.9 %all-to-all-done.1 = f32[8,8,3072]{2,0,1:T(8,128)S(1)} async-done(((f32[8,8,3072]{2,0,1:T(8,128)}), f32[8,8,3072]{2,0,1:T(8,128)S(1)}, u32[]{:S(2)}, u32[]{:S(2)}) %all-to-all-start.1) | async-done | bytes 786464 | tf_op jit(solution)/shard_map/all_to_all | solution.py:84
  352.9 32.4 %all-reduce.3 = (f32[64,64]{1,0:T(8,128)S(1)}, f32[64,64]{1,0:T(8,128)S(1)}) all-reduce(f32[64,64]{1,0:T(8,128)S(1)} %fusion.223, f32[64,64]{1,0:T(8,128)S(1)} %fusion.220), channel_id=2, replica_groups=mesh['gx'=4,'gy'=4,'band'=8] {'band'}, use_global_device_ids=true, to_apply=%region_0.1.clone | all-reduce | flops 8192 | bytes 65536
  385.3 36.4 %all-reduce.2 = (f32[8,64]{1,0:T(8,128)S(1)}, f32[8,64]{1,0:T(8,128)S(1)}) all-reduce(f32[8,64]{1,0:T(8,128)S(1)} %get-tuple-element.168, f32[8,64]{1,0:T(8,128)S(1)} %get-tuple-element.167), channel_id=1, replica_groups=mesh['gx'=4,'gy'=4,'band'=8] {'gx','gy'}, use_global_device_ids=true, to_apply=%region_1.2 | all-reduce | flops 1024 | bytes 8192 | tf_op jit(solution)/shard_map/psum | solution.py:92
  (122 shorter events, 64.0 us)
Async XLA Ops:
  0.6 5.3 %copy-start = (f32[8,8,8,384]{3,2,1,0:T(8,128)S(1)}, f32[8,8,8,384]{3,2,1,0:T(8,128)}, u32[]{:S(2)}) copy-start(f32[8,8,8,384]{3,2,1,0:T(8,128)} %param.2) | copy-start | bytes 2359300
  2.2 12.8 %collective-permute-start.1 = (f32[8,6,8,384]{3,0,2,1:T(8,128)S(1)}, f32[8,6,8,384]{3,0,2,1:T(8,128)S(1)}, u32[]{:S(2)}, u32[]{:S(2)}) collective-permute-start(f32[8,6,8,384]{3,0,2,1:T(8,128)S(1)} %copy.46), channel_id=1, source_target_pairs={{0,32},{32,64},{64,96},{96,0},{1,33},{33,65},{65,97},{97,1},{2,34}... | collective-permute-start | bytes 1769480 | tf_op jit(solution)/shard_map/ppermute | solution.py:31
  2.5 16.8 %collective-permute-start = (f32[8,6,8,384]{3,0,2,1:T(8,128)S(1)}, f32[8,6,8,384]{3,0,2,1:T(8,128)S(1)}, u32[]{:S(2)}, u32[]{:S(2)}) collective-permute-start(f32[8,6,8,384]{3,0,2,1:T(8,128)S(1)} %copy.47), channel_id=1, source_target_pairs={{32,0},{64,32},{96,64},{0,96},{33,1},{65,33},{97,65},{1,97},{34,2}... | collective-permute-start | bytes 1769480 | tf_op jit(solution)/shard_map/ppermute | solution.py:32
  19.7 34.7 %collective-permute-start.2 = (f32[8,20,6,384]{3,0,2,1:T(8,128)S(1)}, f32[8,20,6,384]{3,0,2,1:T(8,128)S(1)}, u32[]{:S(2)}, u32[]{:S(2)}) collective-permute-start(f32[8,20,6,384]{3,0,2,1:T(8,128)S(1)} %get-tuple-element.28), channel_id=1, source_target_pairs={{8,0},{16,8},{24,16},{0,24},{9,1},{17,9},{25,17},{1,25},{10,2},{18... | collective-permute-start | bytes 4423688 | tf_op jit(solution)/shard_map/ppermute | solution.py:32
  20.3 35.5 %collective-permute-start.3 = (f32[8,20,6,384]{3,0,2,1:T(8,128)S(1)}, f32[8,20,6,384]{3,0,2,1:T(8,128)S(1)}, u32[]{:S(2)}, u32[]{:S(2)}) collective-permute-start(f32[8,20,6,384]{3,0,2,1:T(8,128)S(1)} %get-tuple-element.29), channel_id=1, source_target_pairs={{0,8},{8,16},{16,24},{24,0},{1,9},{9,17},{17,25},{25,1},{2,10},{10... | collective-permute-start | bytes 4423688 | tf_op jit(solution)/shard_map/ppermute | solution.py:31
  35.9 3.7 copy-start.1
  54.4 1.4 copy-start.4
  55.8 1.1 copy-start.5
  66.5 13.7 %collective-permute-start.4 = (f32[8,6,8,384]{3,0,2,1:T(8,128)S(1)}, f32[8,6,8,384]{3,0,2,1:T(8,128)S(1)}, u32[]{:S(2)}, u32[]{:S(2)}) collective-permute-start(f32[8,6,8,384]{3,0,2,1:T(8,128)S(1)} %get-tuple-element.132), channel_id=1, source_target_pairs={{32,0},{64,32},{96,64},{0,96},{33,1},{65,33},{97,65},{1,97},{34,2}... | collective-permute-start | bytes 1769480 | tf_op jit(solution)/shard_map/ppermute | solution.py:32
  68.1 16.0 %collective-permute-start.5 = (f32[8,6,8,384]{3,0,2,1:T(8,128)S(1)}, f32[8,6,8,384]{3,0,2,1:T(8,128)S(1)}, u32[]{:S(2)}, u32[]{:S(2)}) collective-permute-start(f32[8,6,8,384]{3,0,2,1:T(8,128)S(1)} %get-tuple-element.133), channel_id=1, source_target_pairs={{0,32},{32,64},{64,96},{96,0},{1,33},{33,65},{65,97},{97,1},{2,34}... | collective-permute-start | bytes 1769480 | tf_op jit(solution)/shard_map/ppermute | solution.py:31
  84.5 33.8 %collective-permute-start.6 = (f32[8,20,6,384]{3,0,2,1:T(8,128)S(1)}, f32[8,20,6,384]{3,0,2,1:T(8,128)S(1)}, u32[]{:S(2)}, u32[]{:S(2)}) collective-permute-start(f32[8,20,6,384]{3,0,2,1:T(8,128)S(1)} %get-tuple-element.26), channel_id=1, source_target_pairs={{8,0},{16,8},{24,16},{0,24},{9,1},{17,9},{25,17},{1,25},{10,2},{18... | collective-permute-start | bytes 4423688 | tf_op jit(solution)/shard_map/ppermute | solution.py:32
  87.5 33.1 %collective-permute-start.7 = (f32[8,20,6,384]{3,0,2,1:T(8,128)S(1)}, f32[8,20,6,384]{3,0,2,1:T(8,128)}, u32[]{:S(2)}, u32[]{:S(2)}) collective-permute-start(f32[8,20,6,384]{3,0,2,1:T(8,128)S(1)} %get-tuple-element.27), channel_id=1, source_target_pairs={{0,8},{8,16},{16,24},{24,0},{1,9},{9,17},{17,25},{25,1},{2,10},{10... | collective-permute-start | bytes 4423688 | tf_op jit(solution)/shard_map/ppermute | solution.py:31
  118.3 1.1 copy-start.6
  134.0 13.4 %collective-permute-start.8 = (f32[8,6,8,384]{3,0,2,1:T(8,128)S(1)}, f32[8,6,8,384]{3,0,2,1:T(8,128)S(1)}, u32[]{:S(2)}, u32[]{:S(2)}) collective-permute-start(f32[8,6,8,384]{3,0,2,1:T(8,128)S(1)} %get-tuple-element.106), channel_id=1, source_target_pairs={{32,0},{64,32},{96,64},{0,96},{33,1},{65,33},{97,65},{1,97},{34,2}... | collective-permute-start | bytes 1769480 | tf_op jit(solution)/shard_map/ppermute | solution.py:32
  134.0 15.2 %collective-permute-start.9 = (f32[8,6,8,384]{3,0,2,1:T(8,128)S(1)}, f32[8,6,8,384]{3,0,2,1:T(8,128)S(1)}, u32[]{:S(2)}, u32[]{:S(2)}) collective-permute-start(f32[8,6,8,384]{3,0,2,1:T(8,128)S(1)} %get-tuple-element.107), channel_id=1, source_target_pairs={{0,32},{32,64},{64,96},{96,0},{1,33},{33,65},{65,97},{97,1},{2,34}... | collective-permute-start | bytes 1769480 | tf_op jit(solution)/shard_map/ppermute | solution.py:31
  149.6 32.9 %collective-permute-start.10 = (f32[8,20,6,384]{3,0,2,1:T(8,128)S(1)}, f32[8,20,6,384]{3,0,2,1:T(8,128)S(1)}, u32[]{:S(2)}, u32[]{:S(2)}) collective-permute-start(f32[8,20,6,384]{3,0,2,1:T(8,128)S(1)} %get-tuple-element.22), channel_id=1, source_target_pairs={{8,0},{16,8},{24,16},{0,24},{9,1},{17,9},{25,17},{1,25},{10,2},{18... | collective-permute-start | bytes 4423688 | tf_op jit(solution)/shard_map/ppermute | solution.py:32
  151.6 32.9 %collective-permute-start.11 = (f32[8,20,6,384]{3,0,2,1:T(8,128)S(1)}, f32[8,20,6,384]{3,0,2,1:T(8,128)}, u32[]{:S(2)}, u32[]{:S(2)}) collective-permute-start(f32[8,20,6,384]{3,0,2,1:T(8,128)S(1)} %get-tuple-element.23), channel_id=1, source_target_pairs={{0,8},{8,16},{16,24},{24,0},{1,9},{9,17},{17,25},{25,1},{2,10},{10... | collective-permute-start | bytes 4423688 | tf_op jit(solution)/shard_map/ppermute | solution.py:31
  182.5 1.1 copy-start.7
  197.5 13.9 %collective-permute-start.12 = (f32[8,6,8,384]{3,0,2,1:T(8,128)S(1)}, f32[8,6,8,384]{3,0,2,1:T(8,128)S(1)}, u32[]{:S(2)}, u32[]{:S(2)}) collective-permute-start(f32[8,6,8,384]{3,0,2,1:T(8,128)S(1)} %get-tuple-element.80), channel_id=1, source_target_pairs={{32,0},{64,32},{96,64},{0,96},{33,1},{65,33},{97,65},{1,97},{34,2}... | collective-permute-start | bytes 1769480 | tf_op jit(solution)/shard_map/ppermute | solution.py:32
  198.8 15.8 %collective-permute-start.13 = (f32[8,6,8,384]{3,0,2,1:T(8,128)S(1)}, f32[8,6,8,384]{3,0,2,1:T(8,128)S(1)}, u32[]{:S(2)}, u32[]{:S(2)}) collective-permute-start(f32[8,6,8,384]{3,0,2,1:T(8,128)S(1)} %get-tuple-element.81), channel_id=1, source_target_pairs={{0,32},{32,64},{64,96},{96,0},{1,33},{33,65},{65,97},{97,1},{2,34}... | collective-permute-start | bytes 1769480 | tf_op jit(solution)/shard_map/ppermute | solution.py:31
  215.0 33.7 %collective-permute-start.14 = (f32[8,20,6,384]{3,0,2,1:T(8,128)S(1)}, f32[8,20,6,384]{3,0,2,1:T(8,128)S(1)}, u32[]{:S(2)}, u32[]{:S(2)}) collective-permute-start(f32[8,20,6,384]{3,0,2,1:T(8,128)S(1)} %get-tuple-element.18), channel_id=1, source_target_pairs={{8,0},{16,8},{24,16},{0,24},{9,1},{17,9},{25,17},{1,25},{10,2},{18... | collective-permute-start | bytes 4423688 | tf_op jit(solution)/shard_map/ppermute | solution.py:32
  217.4 33.8 %collective-permute-start.15 = (f32[8,20,6,384]{3,0,2,1:T(8,128)S(1)}, f32[8,20,6,384]{3,0,2,1:T(8,128)}, u32[]{:S(2)}, u32[]{:S(2)}) collective-permute-start(f32[8,20,6,384]{3,0,2,1:T(8,128)S(1)} %get-tuple-element.19), channel_id=1, source_target_pairs={{0,8},{8,16},{16,24},{24,0},{1,9},{9,17},{17,25},{25,1},{2,10},{10... | collective-permute-start | bytes 4423688 | tf_op jit(solution)/shard_map/ppermute | solution.py:31
  225.5 29.3 %copy-start.2 = (f32[8,8,384]{2,1,0:T(8,128)S(1)}, f32[8,8,384]{2,1,0:T(8,128)}, u32[]{:S(2)}) copy-start(f32[8,8,384]{2,1,0:T(8,128)} %param.3) | copy-start | bytes 294916
  248.7 1.1 copy-start.8
  269.0 12.8 %collective-permute-start.16 = (f32[8,6,8,384]{3,0,2,1:T(8,128)S(1)}, f32[8,6,8,384]{3,0,2,1:T(8,128)S(1)}, u32[]{:S(2)}, u32[]{:S(2)}) collective-permute-start(f32[8,6,8,384]{3,0,2,1:T(8,128)S(1)} %get-tuple-element.54), channel_id=1, source_target_pairs={{32,0},{64,32},{96,64},{0,96},{33,1},{65,33},{97,65},{1,97},{34,2}... | collective-permute-start | bytes 1769480 | tf_op jit(solution)/shard_map/ppermute | solution.py:32
  269.1 15.7 %collective-permute-start.17 = (f32[8,6,8,384]{3,0,2,1:T(8,128)S(1)}, f32[8,6,8,384]{3,0,2,1:T(8,128)S(1)}, u32[]{:S(2)}, u32[]{:S(2)}) collective-permute-start(f32[8,6,8,384]{3,0,2,1:T(8,128)S(1)} %get-tuple-element.55), channel_id=1, source_target_pairs={{0,32},{32,64},{64,96},{96,0},{1,33},{33,65},{65,97},{97,1},{2,34}... | collective-permute-start | bytes 1769480 | tf_op jit(solution)/shard_map/ppermute | solution.py:31
  287.8 33.1 %collective-permute-start.18 = (f32[8,20,6,384]{3,0,2,1:T(8,128)}, f32[8,20,6,384]{3,0,2,1:T(8,128)}, u32[]{:S(2)}, u32[]{:S(2)}) collective-permute-start(f32[8,20,6,384]{3,0,2,1:T(8,128)} %get-tuple-element.14), channel_id=1, source_target_pairs={{8,0},{16,8},{24,16},{0,24},{9,1},{17,9},{25,17},{1,25},{10,2},{18... | collective-permute-start | bytes 4423688 | tf_op jit(solution)/shard_map/ppermute | solution.py:32
  289.4 32.6 %collective-permute-start.19 = (f32[8,20,6,384]{3,0,2,1:T(8,128)}, f32[8,20,6,384]{3,0,2,1:T(8,128)}, u32[]{:S(2)}, u32[]{:S(2)}) collective-permute-start(f32[8,20,6,384]{3,0,2,1:T(8,128)} %get-tuple-element.15), channel_id=1, source_target_pairs={{0,8},{8,16},{16,24},{24,0},{1,9},{9,17},{17,25},{25,1},{2,10},{10... | collective-permute-start | bytes 4423688 | tf_op jit(solution)/shard_map/ppermute | solution.py:31
  291.7 41.9 %all-to-all-start = ((f32[8,8,3072]{2,0,1:T(8,128)}), f32[8,8,3072]{2,0,1:T(8,128)S(1)}, u32[]{:S(2)}, u32[]{:S(2)}) async-start(f32[8,8,3072]{2,0,1:T(8,128)} %bitcast), calls=%async_computation | async-start | bytes 1572864 | tf_op jit(solution)/shard_map/all_to_all | solution.py:83
  311.5 13.3 %copy-start.3 = (f32[8,8,384]{2,1,0:T(8,128)S(1)}, f32[8,8,384]{2,1,0:T(8,128)}, u32[]{:S(2)}) copy-start(f32[8,8,384]{2,1,0:T(8,128)} %param.3) | copy-start | bytes 294916
  324.8 16.2 %copy-start.9 = (u32[128]{0:T(128)S(1)}, u32[128]{0:T(128)}, u32[]{:S(2)}) copy-start(u32[128]{0:T(128)} %constant.37) | copy-start | bytes 1540
  333.7 18.4 %all-to-all-start.1 = ((f32[8,8,3072]{2,0,1:T(8,128)}), f32[8,8,3072]{2,0,1:T(8,128)S(1)}, u32[]{:S(2)}, u32[]{:S(2)}) async-start(f32[8,8,3072]{2,0,1:T(8,128)} %bitcast.4), calls=%async_computation.1 | async-start | bytes 1572864 | tf_op jit(solution)/shard_map/all_to_all | solution.py:84
where the time goes:
time: 427 us; the launch traced here: 423 us
  waiting for transfers between devices  164 us (38%)
  local copies, waits for them, and re-layouts  100 us (23%)
  blocking collectives  68.8 us (16%)
  other arithmetic  53 us (12%)
  starting transfers between devices  33.1 us (8%)
    ppermute x10, waiting for transfers between devices, with_halo(): after = lax.ppermute(leading, axis, down)  132 us
    slice x60, local copies, waits for them, and re-layouts, hamiltonian_apply(): along_z = jnp.roll(field, reach, 3) + jnp.roll(field, -reach, 3)  69.3 us
    psum x1, blocking collectives, per_device(): lax.psum((margin_part, hamilton_part), ('gx', 'gy'))  36.4 us
    unnamed x1, blocking collectives  32.4 us
    ppermute x10, waiting for transfers between devices, with_halo(): before = lax.ppermute(last, axis, up)  25.1 us
    unnamed x51, local copies, waits for them, and re-layouts  25.1 us
    sub x3, other arithmetic, per_device(): 2.0 * (hamiltonian_apply(current, potential) - FILTER_CENTER * current)  20.5 us
    ppermute x10, starting transfers between devices, with_halo(): after = lax.ppermute(leading, axis, down)  15.8 us
  transfers between devices with their start and end apart: 22, of which 21 were waited for; matrix products, arithmetic and copies ran while one was open for 21% of the time, Pallas kernels for 0%

commit v1 on v0

v1 whole, which is shorter than its diff:
```python
import functools

import jax
import jax.numpy as jnp
import ml_dtypes
import numpy as np
from jax import lax
from jax.experimental import pallas as pl
from jax.experimental.pallas import tpu as pltpu
from jax.sharding import PartitionSpec as P

DEGREE = 4

STENCIL_WEIGHTS = (
    -5369.0 / 1800.0,
    12.0 / 7.0,
    -15.0 / 56.0,
    10.0 / 189.0,
    -1.0 / 112.0,
    2.0 / 1925.0,
    -1.0 / 16632.0,
)
GRID_SPACING = 0.5
FILTER_CENTER = 24.0
FILTER_HALFWIDTH = 20.0
KINETIC = -0.5 / (GRID_SPACING * GRID_SPACING)
GRID_AXES = ("gx", "gy")
ALL_AXES = ("band", "gx", "gy")
LANES = 128
HALO = 8
VMEM = pl.BlockSpec(memory_space=pltpu.VMEM)
PARAMS = pltpu.CompilerParams(vmem_limit_bytes=48 * 1024 * 1024)


def lane_index(rows):
    return lax.broadcasted_iota(jnp.int32, (rows, LANES), 1)


def pack_kernel(orb_ref, pot_ref, out_ref):
    lane = lane_index(64)

    def windows(block):
        z0, z1, z2 = (block[:, :, i * LANES : (i + 1) * LANES].reshape(64, LANES) for i in range(3))
        return (
            (z0, jnp.where(lane < 96, z1, z2)),
            (z2, jnp.where(lane < 32, z0, z1)),
        )

    pot = windows(pot_ref[...])
    for j in range(8):
        orb = windows(orb_ref[j])
        for half in range(2):
            for part in range(2):
                out_ref[half * 8 + j, part] = orb[half][part]
                out_ref[half * 8 + j, 2 + part] = pot[half][part]


def band_matrices():
    def circulant(count):
        matrix = np.zeros((count, count), np.float64)
        for reach in range(1, 7):
            for cell in range(count):
                weight = STENCIL_WEIGHTS[reach] / STENCIL_WEIGHTS[1]
                matrix[cell, (cell + reach) % count] += weight
                matrix[cell, (cell - reach) % count] += weight
        return matrix

    def split(matrix):
        high = matrix.astype(ml_dtypes.bfloat16)
        low = (matrix - high.astype(np.float64)).astype(ml_dtypes.bfloat16)
        return high, low

    along_z = split(circulant(256))
    along_y = split(np.kron(np.eye(8), circulant(32)))
    return np.stack(along_z + along_y)


def filter_kernel(half_ref, recv_ref, mat_ref, pack_ref, gram_ref, field_ref, pot_ref):
    half = half_ref[0]
    for gx in range(4):
        for gy in range(4):
            src = gx * 4 + gy
            xs = slice(gx * 8, gx * 8 + 8)
            ys = slice(gy * 8, gy * 8 + 8)
            for part in range(2):
                zs = slice(part * LANES, (part + 1) * LANES)
                piece = recv_ref[src, part].reshape(8, 8, LANES)
                field_ref[0, HALO + gx * 8 : HALO + gx * 8 + 8, ys, zs] = piece
                pot_ref[xs, ys, zs] = recv_ref[src, 2 + part].reshape(8, 8, LANES)

    def wrap(slot):
        field_ref[slot, 0:HALO] = field_ref[slot, 32 : 32 + HALO]
        field_ref[slot, 32 + HALO : 32 + 2 * HALO] = field_ref[slot, HALO : 2 * HALO]

    def apply_group(slot, g):
        x0 = HALO + g * 8
        center = field_ref[slot, pl.ds(x0, 8)]
        flat = center.reshape(256, 256)
        high = flat.astype(jnp.bfloat16)
        low = (flat - high.astype(jnp.float32)).astype(jnp.bfloat16)
        dot = functools.partial(jnp.dot, preferred_element_type=jnp.float32)
        shifts = dot(high, mat_ref[0]) + dot(low, mat_ref[0]) + dot(high, mat_ref[1])
        shifts = shifts + (dot(mat_ref[2], high) + dot(mat_ref[2], low) + dot(mat_ref[3], high))
        shifts = shifts.reshape(8, 32, 256)
        total = (3.0 * STENCIL_WEIGHTS[0] * KINETIC) * center + (
            STENCIL_WEIGHTS[1] * KINETIC
        ) * shifts
        for reach in range(1, 7):
            pair = field_ref[slot, pl.ds(x0 + reach, 8)] + field_ref[slot, pl.ds(x0 - reach, 8)]
            total = total + (STENCIL_WEIGHTS[reach] * KINETIC) * pair
        total = total + pot_ref[pl.ds(g * 8, 8)] * center
        return total, center

    for step in range(DEGREE):
        slot, other = step % 2, (step + 1) % 2
        wrap(slot)

        def advance(g, carry, step=step, slot=slot, other=other):
            applied, center = apply_group(slot, g)
            rows = pl.ds(HALO + g * 8, 8)
            if step == 0:
                following = (applied - FILTER_CENTER * center) * (1.0 / FILTER_HALFWIDTH)
            else:
                following = (applied - FILTER_CENTER * center) * (
                    2.0 / FILTER_HALFWIDTH
                ) - field_ref[other, rows]
            field_ref[other, rows] = following
            return carry

        lax.fori_loop(0, 4, advance, 0)

    slot = DEGREE % 2
    wrap(slot)
    own32 = (lane_index(32) < 64) == (half == 0)
    own8 = ((lax.broadcasted_iota(jnp.int32, (32, 8, LANES), 2) < 64)) == (half == 0)

    def finish(g, carry):
        applied, center = apply_group(slot, g)
        for gy in range(4):
            ys = slice(gy * 8, gy * 8 + 8)
            main = center[:, ys, :LANES].reshape(64, LANES)
            rest = center[:, ys, LANES:].reshape(64, LANES)
            joined = jnp.where(own32, rest[:32], pltpu.roll(rest[32:], 64, 1))
            pack_ref[g * 4 + gy, :64] = main
            pack_ref[g * 4 + gy, 64:] = joined
        tiles = center.reshape(32, 8, 256)
        applied_tiles = applied.reshape(32, 8, 256)
        moved = pltpu.roll(applied_tiles[:, :, LANES:].reshape(256, LANES), 64, 1).reshape(32, 8, LANES)
        rows = pl.ds(g * 32, 32)
        gram_ref[rows, 0:8] = tiles[:, :, :LANES]
        gram_ref[rows, 8:16] = applied_tiles[:, :, :LANES]
        gram_ref[rows, 16:24] = jnp.where(own8, tiles[:, :, LANES:], moved)
        return carry

    lax.fori_loop(0, 4, finish, 0)


def unpack_kernel(recv_ref, out_ref):
    lane = lane_index(32)
    for j in range(8):
        zero, one = recv_ref[j], recv_ref[8 + j]
        out_ref[j, :, :, :LANES] = zero[:64].reshape(8, 8, LANES)
        out_ref[j, :, :, 2 * LANES :] = one[:64].reshape(8, 8, LANES)
        first = jnp.where(lane < 64, zero[64:], one[64:])
        second = pltpu.roll(jnp.where(lane < 64, one[64:], zero[64:]), 64, 1)
        out_ref[j, :4, :, LANES : 2 * LANES] = first.reshape(4, 8, LANES)
        out_ref[j, 4:, :, LANES : 2 * LANES] = second.reshape(4, 8, LANES)


def gram_kernel(recv_ref, out_ref):
    lane = lane_index(64)

    def rows_of(half, k):
        parts = [recv_ref[pl.ds((b * 2 + half) * 8 * 24 + k, 8, stride=24), :] for b in range(8)]
        return jnp.concatenate(parts, axis=0)

    def split(pieces):
        whole = jnp.concatenate(pieces, axis=1)
        high = whole.astype(jnp.bfloat16)
        low = (whole - high.astype(jnp.float32)).astype(jnp.bfloat16)
        return high, low

    total = jnp.zeros((128, 256), jnp.float32)
    for k in range(8):
        rest0, rest1 = rows_of(0, 16 + k), rows_of(1, 16 + k)
        rest = jnp.where(lane < 64, rest0, rest1)
        rest_applied = pltpu.roll(jnp.where(lane < 64, rest1, rest0), 64, 1)
        f1, f2 = split([rows_of(0, k), rows_of(1, k), rest])
        a1, a2 = split([rows_of(0, 8 + k), rows_of(1, 8 + k), rest_applied])
        total = total + lax.dot_general(
            jnp.concatenate([f1, f2], axis=0),
            jnp.concatenate([f1, a1, f2, a2], axis=0),
            (((1,), (1,)), ((), ())),
            preferred_element_type=jnp.float32,
        )
    total = total[:64] + total[64:]
    total = total[:, :LANES] + total[:, LANES:]
    for b in range(8):
        rows = total[b * 8 : b * 8 + 8]
        out_ref[b] = jnp.broadcast_to(rows[None], (16, 8, LANES))


def sum_kernel(recv_ref, margin_ref, hamiltonian_ref, *, scale):
    total = jnp.sum(recv_ref[...], axis=0) * scale
    margin_ref[...] = total[:, :64]
    hamiltonian_ref[...] = pltpu.roll(total, 64, 1)[:, :64]


def call(kernel, shapes, *args, scratch=(), smem=0):
    single = not isinstance(shapes, list)
    outs = [jax.ShapeDtypeStruct(s, jnp.float32) for s in ([shapes] if single else shapes)]
    specs = [pl.BlockSpec(memory_space=pltpu.SMEM)] * smem + [VMEM] * (len(args) - smem)
    result = pl.pallas_call(
        kernel,
        out_shape=outs[0] if single else outs,
        in_specs=specs,
        out_specs=VMEM if single else [VMEM] * len(outs),
        scratch_shapes=list(scratch),
        compiler_params=PARAMS,
    )(*args)
    return result


def exchange(array, axes):
    return lax.all_to_all(array, axes, split_axis=0, concat_axis=0, tiled=True)


def per_device(orbitals, potential):
    packed = call(pack_kernel, (16, 4, 64, LANES), orbitals, potential)
    windows = exchange(packed, GRID_AXES)
    half = (lax.axis_index("gx") // 2).astype(jnp.int32).reshape(1)
    matrices = jnp.asarray(band_matrices())
    pieces, gram_pieces = call(
        filter_kernel,
        [(16, 96, LANES), (128, 24, LANES)],
        half,
        windows,
        matrices,
        scratch=(
            pltpu.VMEM((2, 32 + 2 * HALO, 32, 256), jnp.float32),
            pltpu.VMEM((32, 32, 256), jnp.float32),
        ),
        smem=1,
    )
    gram_cells = exchange(gram_pieces, ALL_AXES)
    partial = call(gram_kernel, (8, 16, 8, LANES), gram_cells.reshape(128 * 24, LANES))
    filtered = call(unpack_kernel, (8, 8, 8, 384), exchange(pieces, GRID_AXES))
    sums = exchange(partial.reshape(128, 8, LANES), ALL_AXES)
    scale = 1.0 / (8 * 8 * 384)
    margin, hamiltonian = call(
        functools.partial(sum_kernel, scale=scale), [(8, 64), (8, 64)], sums
    )
    return filtered, margin, hamiltonian


def solution(mesh):
    placed = (P("band", "gx", "gy", None), P("gx", "gy", None))
    return jax.shard_map(
        per_device,
        mesh=mesh,
        in_specs=placed,
        out_specs=(P("band", "gx", "gy", None), P("band", None), P("band", None)),
        check_vma=False,
    )
```

time: 427 us -> 124 us (0.29)
  the two profiles are of different devices: /device:TPU:2 before, /device:TPU:1 now
where the time goes in v1:
time: 124 us; the launch traced here: 123 us
  waiting for transfers between devices  52.9 us (43%)
  blocking collectives  30.5 us (25%)
  starting transfers between devices  19.8 us (16%)
  Pallas kernels  16.2 us (13%)
  local copies, waits for them, and re-layouts  3.34 us (3%)
    all_to_all x3, waiting for transfers between devices, exchange(): return lax.all_to_all(array, axes, split_axis=0, concat_axis=0, tiled=True)  52.9 us
    all_to_all x1, blocking collectives, exchange(): return lax.all_to_all(array, axes, split_axis=0, concat_axis=0, tiled=True)  30.5 us
    all_to_all x3, starting transfers between devices, exchange(): return lax.all_to_all(array, axes, split_axis=0, concat_axis=0, tiled=True)  19.8 us
    pallas_call x5, Pallas kernels, call(): pl.pallas_call(kernel, out_shape=outs[0] if single else outs, in_specs=sp...  16.2 us
    unnamed x8, local copies, waits for them, and re-layouts  3.34 us
  transfers between devices with their start and end apart: 3, of which 3 were waited for; matrix products, arithmetic and copies ran while one was open for 0% of the time, Pallas kernels for 2%

profile of v1, /device:TPU:1, one launch (start us, length us, event | category | flops | bytes accessed | tf_op | source)
XLA Modules:
  0.0 123.4 jit_solution(3729264166927628330)
XLA Ops:
  0.6 0.0 copy-start.1
  0.6 1.1 copy-done.1
  1.8 0.0 copy-start.3
  1.8 0.9 copy-done.3
  2.7 0.1 shard_map.58
  2.8 0.0 copy-start
  2.8 1.3 %copy-done = f32[16,4,64,128]{3,2,1,0:T(8,128)} copy-done((f32[16,4,64,128]{3,2,1,0:T(8,128)}, f32[16,4,64,128]{3,2,1,0:T(8,128)S(1)}, u32[]{:S(2)}) %copy-start) | copy-done | bytes 2097176
  4.1 0.0 copy-start.2
  4.1 9.3 %all-to-all-start = ((f32[16,4,64,128]{3,2,1,0:T(8,128)}), f32[16,4,64,128]{3,2,1,0:T(8,128)S(1)}, u32[]{:S(2)}, u32[]{:S(2)}) async-start(f32[16,4,64,128]{3,2,1,0:T(8,128)} %copy-done), calls=%async_computation | async-start | bytes 4194304 | tf_op jit(solution)/shard_map/all_to_all | solution.py:225
  13.4 29.0 %all-to-all-done.recv_ref = f32[16,4,64,128]{3,2,1,0:T(8,128)S(1)} async-done(((f32[16,4,64,128]{3,2,1,0:T(8,128)}), f32[16,4,64,128]{3,2,1,0:T(8,128)S(1)}, u32[]{:S(2)}, u32[]{:S(2)}) %all-to-all-start) | async-done | bytes 2097184 | tf_op jit(solution)/shard_map/all_to_all | solution.py:225
  42.5 0.0 copy-done.2
  42.5 12.8 %shard_map.59 = (f32[16,96,128]{2,1,0:T(8,128)}, f32[128,24,128]{2,1,0:T(8,128)S(1)}) custom-call(s32[1]{0:T(128)} %bitcast.half_ref, f32[16,4,64,128]{3,2,1,0:T(8,128)S(1)} %all-to-all-done.recv_ref, bf16[4,256,256]{2,1,0:T(8,128)(2,1)S(1)} %copy-done.2), custom_call_target="tpu_custom_call" | custom-call | tf_op jit(solution)/shard_map/pallas_call | solution.py:213
  55.2 30.5 %all_to_all.20 = f32[128,24,128]{2,1,0:T(8,128)S(1)} all-to-all(f32[128,24,128]{2,1,0:T(8,128)S(1)} %get-tuple-element.8), channel_id=1, replica_groups=mesh['gx'=4,'gy'=4,'band'=8] {'band','gx','gy'}, dimensions={0} | all-to-all | bytes 3145728 | tf_op jit(solution)/shard_map/all_to_all | solution.py:225
  85.7 4.5 %all-to-all-start.1 = ((f32[16,96,128]{2,1,0:T(8,128)}), f32[16,96,128]{2,1,0:T(8,128)S(1)}, u32[]{:S(2)}, u32[]{:S(2)}) async-start(f32[16,96,128]{2,1,0:T(8,128)} %get-tuple-element.7), calls=%async_computation.1 | async-start | bytes 1572864 | tf_op jit(solution)/shard_map/all_to_all | solution.py:225
  90.2 1.5 %shard_map.61 = f32[8,16,8,128]{3,2,1,0:T(8,128)} custom-call(f32[3072,128]{1,0:T(8,128)S(1)} %bitcast.3), custom_call_target="tpu_custom_call" | custom-call | tf_op jit(solution)/shard_map/pallas_call | solution.py:213
  91.7 11.3 %all-to-all-done.1.recv_ref = f32[16,96,128]{2,1,0:T(8,128)S(1)} async-done(((f32[16,96,128]{2,1,0:T(8,128)}), f32[16,96,128]{2,1,0:T(8,128)S(1)}, u32[]{:S(2)}, u32[]{:S(2)}) %all-to-all-start.1) | async-done | bytes 786464 | tf_op jit(solution)/shard_map/all_to_all | solution.py:225
  103.0 6.0 %all-to-all-start.3 = ((f32[128,8,128]{2,1,0:T(8,128)}), f32[128,8,128]{2,1,0:T(8,128)S(1)}, u32[]{:S(2)}, u32[]{:S(2)}) async-start(f32[128,8,128]{2,1,0:T(8,128)} %bitcast.2), calls=%async_computation.3 | async-start | bytes 1048576 | tf_op jit(solution)/shard_map/all_to_all | solution.py:225
  109.0 1.0 shard_map.60
  110.0 12.5 %all-to-all-done.3.recv_ref = f32[128,8,128]{2,1,0:T(8,128)S(1)} async-done(((f32[128,8,128]{2,1,0:T(8,128)}), f32[128,8,128]{2,1,0:T(8,128)S(1)}, u32[]{:S(2)}, u32[]{:S(2)}) %all-to-all-start.3) | async-done | bytes 524320 | tf_op jit(solution)/shard_map/all_to_all | solution.py:225
  122.6 0.8 shard_map.62
Async XLA Ops:
  0.6 1.1 copy-start.1
  1.8 0.9 copy-start.3
  2.8 1.3 %copy-start = (f32[16,4,64,128]{3,2,1,0:T(8,128)}, f32[16,4,64,128]{3,2,1,0:T(8,128)S(1)}, u32[]{:S(2)}) copy-start(f32[16,4,64,128]{3,2,1,0:T(8,128)S(1)} %shard_map.58) | copy-start | bytes 6291460
  4.1 38.3 %copy-start.2 = (bf16[4,256,256]{2,1,0:T(8,128)(2,1)S(1)}, bf16[4,256,256]{2,1,0:T(8,128)(2,1)}, u32[]{:S(2)}) copy-start(bf16[4,256,256]{2,1,0:T(8,128)(2,1)} %constant.22.clone.mat_ref) | copy-start | bytes 1572868
  4.1 38.3 %all-to-all-start = ((f32[16,4,64,128]{3,2,1,0:T(8,128)}), f32[16,4,64,128]{3,2,1,0:T(8,128)S(1)}, u32[]{:S(2)}, u32[]{:S(2)}) async-start(f32[16,4,64,128]{3,2,1,0:T(8,128)} %copy-done), calls=%async_computation | async-start | bytes 4194304 | tf_op jit(solution)/shard_map/all_to_all | solution.py:225
  85.7 17.3 %all-to-all-start.1 = ((f32[16,96,128]{2,1,0:T(8,128)}), f32[16,96,128]{2,1,0:T(8,128)S(1)}, u32[]{:S(2)}, u32[]{:S(2)}) async-start(f32[16,96,128]{2,1,0:T(8,128)} %get-tuple-element.7), calls=%async_computation.1 | async-start | bytes 1572864 | tf_op jit(solution)/shard_map/all_to_all | solution.py:225
  103.0 19.6 %all-to-all-start.3 = ((f32[128,8,128]{2,1,0:T(8,128)}), f32[128,8,128]{2,1,0:T(8,128)S(1)}, u32[]{:S(2)}, u32[]{:S(2)}) async-start(f32[128,8,128]{2,1,0:T(8,128)} %bitcast.2), calls=%async_computation.3 | async-start | bytes 1048576 | tf_op jit(solution)/shard_map/all_to_all | solution.py:225

commit v2 on v1

--- a/solution.py
+++ b/solution.py
@@ -75,7 +75,7 @@
     return np.stack(along_z + along_y)
 
 
-def filter_kernel(half_ref, recv_ref, mat_ref, pack_ref, gram_ref, field_ref, pot_ref):
+def filter_kernel(half_ref, recv_ref, mat_ref, gram_ref, field_ref, pot_ref):
     half = half_ref[0]
     for gx in range(4):
         for gy in range(4):
@@ -131,40 +131,21 @@
 
     slot = DEGREE % 2
     wrap(slot)
-    own32 = (lane_index(32) < 64) == (half == 0)
-    own8 = ((lax.broadcasted_iota(jnp.int32, (32, 8, LANES), 2) < 64)) == (half == 0)
+    own = (lax.broadcasted_iota(jnp.int32, (8, 4, 8, LANES), 3) < 64) == (half == 0)
 
     def finish(g, carry):
         applied, center = apply_group(slot, g)
-        for gy in range(4):
-            ys = slice(gy * 8, gy * 8 + 8)
-            main = center[:, ys, :LANES].reshape(64, LANES)
-            rest = center[:, ys, LANES:].reshape(64, LANES)
-            joined = jnp.where(own32, rest[:32], pltpu.roll(rest[32:], 64, 1))
-            pack_ref[g * 4 + gy, :64] = main
-            pack_ref[g * 4 + gy, 64:] = joined
-        tiles = center.reshape(32, 8, 256)
-        applied_tiles = applied.reshape(32, 8, 256)
-        moved = pltpu.roll(applied_tiles[:, :, LANES:].reshape(256, LANES), 64, 1).reshape(32, 8, LANES)
-        rows = pl.ds(g * 32, 32)
-        gram_ref[rows, 0:8] = tiles[:, :, :LANES]
-        gram_ref[rows, 8:16] = applied_tiles[:, :, :LANES]
-        gram_ref[rows, 16:24] = jnp.where(own8, tiles[:, :, LANES:], moved)
+        tiles = center.reshape(8, 4, 8, 256)
+        applied_tiles = applied.reshape(8, 4, 8, 256)
+        moved = pltpu.roll(applied_tiles[..., LANES:].reshape(256, LANES), 64, 1)
+        gram_ref[:, g, :, 0:8] = tiles[..., :LANES]
+        gram_ref[:, g, :, 8:16] = applied_tiles[..., :LANES]
+        gram_ref[:, g, :, 16:24] = jnp.where(
+            own, tiles[..., LANES:], moved.reshape(8, 4, 8, LANES)
+        )
         return carry
 
     lax.fori_loop(0, 4, finish, 0)
-
-
-def unpack_kernel(recv_ref, out_ref):
-    lane = lane_index(32)
-    for j in range(8):
-        zero, one = recv_ref[j], recv_ref[8 + j]
-        out_ref[j, :, :, :LANES] = zero[:64].reshape(8, 8, LANES)
-        out_ref[j, :, :, 2 * LANES :] = one[:64].reshape(8, 8, LANES)
-        first = jnp.where(lane < 64, zero[64:], one[64:])
-        second = pltpu.roll(jnp.where(lane < 64, one[64:], zero[64:]), 64, 1)
-        out_ref[j, :4, :, LANES : 2 * LANES] = first.reshape(4, 8, LANES)
-        out_ref[j, 4:, :, LANES : 2 * LANES] = second.reshape(4, 8, LANES)
 
 
 def gram_kernel(recv_ref, out_ref):
@@ -195,9 +176,27 @@
         )
     total = total[:64] + total[64:]
     total = total[:, :LANES] + total[:, LANES:]
+    near = lane_index(8) < 64
     for b in range(8):
-        rows = total[b * 8 : b * 8 + 8]
-        out_ref[b] = jnp.broadcast_to(rows[None], (16, 8, LANES))
+        for j in range(8):
+            zero, one = (((b * 2 + h) * 8 + j) * 24 for h in range(2))
+            rest = jnp.where(near, recv_ref[zero + 16 : zero + 24], recv_ref[one + 16 : one + 24])
+            out_ref[b, j * 8 : j * 8 + 8] = recv_ref[zero : zero + 8]
+            out_ref[b, 64 + j * 8 : 64 + j * 8 + 8] = rest
+            out_ref[b, 128 + j * 8 : 128 + j * 8 + 8] = recv_ref[one : one + 8]
+        out_ref[b, 192:200] = total[b * 8 : b * 8 + 8]
+
+
+def band_sum_kernel(recv_ref, out_ref):
+    total = jnp.sum(recv_ref[:, 192:200], axis=0)
+    out_ref[...] = jnp.broadcast_to(total[None], (16, 8, LANES))
+
+
+def unpack_kernel(recv_ref, out_ref):
+    for x in range(8):
+        for part in range(3):
+            piece = recv_ref[x, part * 64 : part * 64 + 64].reshape(8, 8, LANES)
+            out_ref[:, x, :, part * LANES : (part + 1) * LANES] = piece
 
 
 def sum_kernel(recv_ref, margin_ref, hamiltonian_ref, *, scale):
@@ -230,9 +229,9 @@
     windows = exchange(packed, GRID_AXES)
     half = (lax.axis_index("gx") // 2).astype(jnp.int32).reshape(1)
     matrices = jnp.asarray(band_matrices())
-    pieces, gram_pieces = call(
+    rows = call(
         filter_kernel,
-        [(16, 96, LANES), (128, 24, LANES)],
+        (8, 4, 4, 24, LANES),
         half,
         windows,
         matrices,
@@ -242,10 +241,11 @@
         ),
         smem=1,
     )
-    gram_cells = exchange(gram_pieces, ALL_AXES)
-    partial = call(gram_kernel, (8, 16, 8, LANES), gram_cells.reshape(128 * 24, LANES))
-    filtered = call(unpack_kernel, (8, 8, 8, 384), exchange(pieces, GRID_AXES))
-    sums = exchange(partial.reshape(128, 8, LANES), ALL_AXES)
+    cells = exchange(rows.reshape(128, 24, LANES), ALL_AXES)
+    outgoing = call(gram_kernel, (8, 200, LANES), cells.reshape(128 * 24, LANES))
+    home = exchange(outgoing, "band")
+    sums = exchange(call(band_sum_kernel, (16, 8, LANES), home), GRID_AXES)
+    filtered = call(unpack_kernel, (8, 8, 8, 384), home)
     scale = 1.0 / (8 * 8 * 384)
     margin, hamiltonian = call(
         functools.partial(sum_kernel, scale=scale), [(8, 64), (8, 64)], sums

time: 124 us -> 116 us (0.935)
  waiting for transfers between devices: 52.9 us -> 35.5 us
  blocking collectives: 30.5 us -> 47.5 us
  starting transfers between devices: 19.8 us -> 13.6 us
    all_to_all x3 -> x2, waiting for transfers between devices: 52.9 us -> 35.5 us  [exchange(): return lax.all_to_all(array, axes, split_axis=0, concat_axis=0, tiled=True)]
    all_to_all x1 -> x2, blocking collectives: 30.5 us -> 47.5 us  [exchange(): return lax.all_to_all(array, axes, split_axis=0, concat_axis=0, tiled=True)]
    all_to_all x3 -> x2, starting transfers between devices: 19.8 us -> 13.6 us  [exchange(): return lax.all_to_all(array, axes, split_axis=0, concat_axis=0, tiled=True)]
    pallas_call x5 -> x6, Pallas kernels: 16.2 us -> 15 us  [call(): pl.pallas_call(kernel, out_shape=outs[0] if single else outs, in_specs=sp...]
  transfers between devices with their start and end apart: 3 -> 2, of which waited for: 3 -> 2; matrix products, arithmetic and copies ran while one was open for 0% -> 0% of each run, Pallas kernels for 2% -> 1%
where the time goes in v2:
time: 116 us
  blocking collectives  47.5 us (41%)
  waiting for transfers between devices  35.5 us (31%)
  Pallas kernels  15 us (13%)
  starting transfers between devices  13.6 us (12%)
  local copies, waits for them, and re-layouts  3.36 us (3%)
    all_to_all x2, blocking collectives, exchange(): return lax.all_to_all(array, axes, split_axis=0, concat_axis=0, tiled=True)  47.5 us
    all_to_all x2, waiting for transfers between devices, exchange(): return lax.all_to_all(array, axes, split_axis=0, concat_axis=0, tiled=True)  35.5 us
    pallas_call x6, Pallas kernels, call(): pl.pallas_call(kernel, out_shape=outs[0] if single else outs, in_specs=sp...  15 us
    all_to_all x2, starting transfers between devices, exchange(): return lax.all_to_all(array, axes, split_axis=0, concat_axis=0, tiled=True)  13.6 us
    unnamed x8, local copies, waits for them, and re-layouts  3.36 us
  transfers between devices with their start and end apart: 2, of which 2 were waited for; matrix products, arithmetic and copies ran while one was open for 0% of the time, Pallas kernels for 1%

profile of v2, /device:TPU:1, one launch (start us, length us, event | category | flops | bytes accessed | tf_op | source)
XLA Modules:
  0.0 115.6 jit_solution(7827022934702390420)
XLA Ops:
  0.6 0.0 copy-start.1
  0.6 1.1 copy-done.1
  1.8 0.0 copy-start.3
  1.8 0.9 copy-done.3
  2.7 0.1 shard_map.58
  2.8 0.0 copy-start
  2.8 1.3 %copy-done = f32[16,4,64,128]{3,2,1,0:T(8,128)} copy-done((f32[16,4,64,128]{3,2,1,0:T(8,128)}, f32[16,4,64,128]{3,2,1,0:T(8,128)S(1)}, u32[]{:S(2)}) %copy-start) | copy-done | bytes 2097176
  4.2 0.0 copy-start.2
  4.2 9.3 %all-to-all-start = ((f32[16,4,64,128]{3,2,1,0:T(8,128)}), f32[16,4,64,128]{3,2,1,0:T(8,128)S(1)}, u32[]{:S(2)}, u32[]{:S(2)}) async-start(f32[16,4,64,128]{3,2,1,0:T(8,128)} %copy-done), calls=%async_computation | async-start | bytes 4194304 | tf_op jit(solution)/shard_map/all_to_all | solution.py:224
  13.4 29.0 %all-to-all-done.recv_ref = f32[16,4,64,128]{3,2,1,0:T(8,128)S(1)} async-done(((f32[16,4,64,128]{3,2,1,0:T(8,128)}), f32[16,4,64,128]{3,2,1,0:T(8,128)S(1)}, u32[]{:S(2)}, u32[]{:S(2)}) %all-to-all-start) | async-done | bytes 2097184 | tf_op jit(solution)/shard_map/all_to_all | solution.py:224
  42.5 0.0 copy-done.2
  42.5 11.9 %shard_map.59 = f32[8,4,4,24,128]{4,3,2,1,0:T(8,128)S(1)} custom-call(s32[1]{0:T(128)} %bitcast.half_ref, f32[16,4,64,128]{3,2,1,0:T(8,128)S(1)} %all-to-all-done.recv_ref, bf16[4,256,256]{2,1,0:T(8,128)(2,1)S(1)} %copy-done.2), custom_call_target="tpu_custom_call" | custom-call | tf_op jit(solution)/shard_map/pallas_call | solution.py:212
  54.4 30.5 %all_to_all.20 = f32[128,24,128]{2,1,0:T(8,128)S(1)} all-to-all(f32[128,24,128]{2,1,0:T(8,128)S(1)} %bitcast.3), channel_id=1, replica_groups=mesh['gx'=4,'gy'=4,'band'=8] {'band','gx','gy'}, dimensions={0} | all-to-all | bytes 3145728 | tf_op jit(solution)/shard_map/all_to_all | solution.py:224
  84.9 0.7 shard_map.60
  85.6 16.9 %all_to_all.21.recv_ref = f32[8,200,128]{2,1,0:T(8,128)S(1)} all-to-all(f32[8,200,128]{2,1,0:T(8,128)S(1)} %shard_map.60), channel_id=1, replica_groups=mesh['gx'=4,'gy'=4,'band'=8] {'band'}, dimensions={0} | all-to-all | bytes 1638400 | tf_op jit(solution)/shard_map/all_to_all | solution.py:224
  102.6 0.6 shard_map.62
  103.2 4.4 %all-to-all-start.3 = ((f32[16,8,128]{2,1,0:T(8,128)}), f32[16,8,128]{2,1,0:T(8,128)S(1)}, u32[]{:S(2)}, u32[]{:S(2)}) async-start(f32[16,8,128]{2,1,0:T(8,128)} %shard_map.62), calls=%async_computation.3 | async-start | bytes 131072 | tf_op jit(solution)/shard_map/all_to_all | solution.py:224
  107.6 0.9 shard_map.61
  108.5 6.4 %all-to-all-done.3.recv_ref = f32[16,8,128]{2,1,0:T(8,128)S(1)} async-done(((f32[16,8,128]{2,1,0:T(8,128)}), f32[16,8,128]{2,1,0:T(8,128)S(1)}, u32[]{:S(2)}, u32[]{:S(2)}) %all-to-all-start.3) | async-done | bytes 65568 | tf_op jit(solution)/shard_map/all_to_all | solution.py:224
  115.0 0.7 shard_map.63
Async XLA Ops:
  0.6 1.1 copy-start.1
  1.8 0.9 copy-start.3
  2.8 1.3 %copy-start = (f32[16,4,64,128]{3,2,1,0:T(8,128)}, f32[16,4,64,128]{3,2,1,0:T(8,128)S(1)}, u32[]{:S(2)}) copy-start(f32[16,4,64,128]{3,2,1,0:T(8,128)S(1)} %shard_map.58) | copy-start | bytes 6291460
  4.2 38.3 %copy-start.2 = (bf16[4,256,256]{2,1,0:T(8,128)(2,1)S(1)}, bf16[4,256,256]{2,1,0:T(8,128)(2,1)}, u32[]{:S(2)}) copy-start(bf16[4,256,256]{2,1,0:T(8,128)(2,1)} %constant.22.clone.mat_ref) | copy-start | bytes 1572868
  4.2 38.3 %all-to-all-start = ((f32[16,4,64,128]{3,2,1,0:T(8,128)}), f32[16,4,64,128]{3,2,1,0:T(8,128)S(1)}, u32[]{:S(2)}, u32[]{:S(2)}) async-start(f32[16,4,64,128]{3,2,1,0:T(8,128)} %copy-done), calls=%async_computation | async-start | bytes 4194304 | tf_op jit(solution)/shard_map/all_to_all | solution.py:224
  103.2 11.7 %all-to-all-start.3 = ((f32[16,8,128]{2,1,0:T(8,128)}), f32[16,8,128]{2,1,0:T(8,128)S(1)}, u32[]{:S(2)}, u32[]{:S(2)}) async-start(f32[16,8,128]{2,1,0:T(8,128)} %shard_map.62), calls=%async_computation.3 | async-start | bytes 131072 | tf_op jit(solution)/shard_map/all_to_all | solution.py:224

commit v3 on v2

--- a/solution.py
+++ b/solution.py
@@ -24,6 +24,7 @@
 FILTER_CENTER = 24.0
 FILTER_HALFWIDTH = 20.0
 KINETIC = -0.5 / (GRID_SPACING * GRID_SPACING)
+STEP = 2.0 / FILTER_HALFWIDTH
 GRID_AXES = ("gx", "gy")
 ALL_AXES = ("band", "gx", "gy")
 LANES = 128
@@ -36,7 +37,11 @@
     return lax.broadcasted_iota(jnp.int32, (rows, LANES), 1)
 
 
-def pack_kernel(orb_ref, pot_ref, out_ref):
+def pack_kernel(orb_ref, pot_ref, out_ref, orb, pot, packed, in_sems, out_sems):
+    loads = [pltpu.make_async_copy(pot_ref, pot, in_sems.at[8])]
+    loads += [pltpu.make_async_copy(orb_ref.at[j], orb.at[j], in_sems.at[j]) for j in range(8)]
+    for load in loads:
+        load.start()
     lane = lane_index(64)
 
     def windows(block):
@@ -46,13 +51,24 @@
             (z2, jnp.where(lane < 32, z0, z1)),
         )
 
-    pot = windows(pot_ref[...])
+    loads[0].wait()
+    pot_windows = windows(pot[...])
+    for half in range(2):
+        for j in range(8):
+            packed[half, j, 2] = pot_windows[half][j // 4]
+    stores = []
     for j in range(8):
-        orb = windows(orb_ref[j])
+        loads[1 + j].wait()
+        orb_windows = windows(orb[j])
         for half in range(2):
             for part in range(2):
-                out_ref[half * 8 + j, part] = orb[half][part]
-                out_ref[half * 8 + j, 2 + part] = pot[half][part]
+                packed[half, j, part] = orb_windows[half][part]
+        stores.append(
+            pltpu.make_async_copy(packed.at[:, j], out_ref.at[:, j], out_sems.at[j])
+        )
+        stores[-1].start()
+    for store in stores:
+        store.wait()
 
 
 def band_matrices():
@@ -70,82 +86,102 @@
         low = (matrix - high.astype(np.float64)).astype(ml_dtypes.bfloat16)
         return high, low
 
-    along_z = split(circulant(256))
-    along_y = split(np.kron(np.eye(8), circulant(32)))
-    return np.stack(along_z + along_y)
-
-
-def filter_kernel(half_ref, recv_ref, mat_ref, gram_ref, field_ref, pot_ref):
-    half = half_ref[0]
+    z_high, z_low = split(circulant(256))
+    y_high, y_low = split(np.kron(np.eye(8), circulant(32)))
+    return np.concatenate([z_high, z_high, z_low]), np.concatenate(
+        [y_high[:128, :128], y_high[:128, :128]], axis=1
+    ), y_low
+
+
+def kinetic_group(field_ref, mats, g):
+    z_ref, y_ref, y_low_ref = mats
+    x0 = HALO + g * 8
+    center = field_ref[x0 : x0 + 8]
+    flat = center.reshape(256, 256)
+    high = flat.astype(jnp.bfloat16)
+    low = (flat - high.astype(jnp.float32)).astype(jnp.bfloat16)
+    dot = functools.partial(jnp.dot, preferred_element_type=jnp.float32)
+    shifts = dot(jnp.concatenate([high, low, high], axis=1), z_ref[...])
+    along_y = [
+        dot(y_ref[...], jnp.concatenate([high[rows], low[rows]], axis=0))
+        for rows in (slice(0, 128), slice(128, 256))
+    ]
+    shifts = shifts + jnp.concatenate(along_y, axis=0) + dot(y_low_ref[...], high)
+    total = (STENCIL_WEIGHTS[1] * KINETIC * STEP) * shifts.reshape(8, 32, 256)
+    for reach in range(1, 7):
+        pair = field_ref[x0 + reach : x0 + reach + 8] + field_ref[x0 - reach : x0 - reach + 8]
+        total = total + (STENCIL_WEIGHTS[reach] * KINETIC * STEP) * pair
+    return total, center
+
+
+def wrap(field_ref):
+    field_ref[0:HALO] = field_ref[32 : 32 + HALO]
+    field_ref[32 + HALO : 32 + 2 * HALO] = field_ref[HALO : 2 * HALO]
+
+
+def domain(gx, gy):
+    return gx * 4 + gy, slice(gx * 8, gx * 8 + 8), slice(gy * 8, gy * 8 + 8)
+
+
+def kinetic_kernel(recv_ref, z_ref, y_ref, y_low_ref, out_ref, field_ref):
     for gx in range(4):
         for gy in range(4):
-            src = gx * 4 + gy
-            xs = slice(gx * 8, gx * 8 + 8)
-            ys = slice(gy * 8, gy * 8 + 8)
+            src, xs, ys = domain(gx, gy)
+            for part in range(2):
+                piece = recv_ref[src, part].reshape(8, 8, LANES)
+                zs = slice(part * LANES, (part + 1) * LANES)
+                field_ref[HALO + gx * 8 : HALO + gx * 8 + 8, ys, zs] = piece
+    wrap(field_ref)
+    for g in range(4):
+        out_ref[g * 8 : g * 8 + 8], _ = kinetic_group(field_ref, (z_ref, y_ref, y_low_ref), g)
+
+
+def filter_kernel(
+    place_ref, recv_ref, other_ref, first_ref, z_ref, y_ref, y_low_ref, out_ref, even_ref, odd_ref, pot_ref
+):
+    half, core = place_ref[0], place_ref[1]
+    mats = (z_ref, y_ref, y_low_ref)
+    for gx in range(4):
+        for gy in range(4):
+            src, xs, ys = domain(gx, gy)
+            mine = recv_ref[src, 2]
+            theirs = other_ref[src]
+            rows = slice(HALO + gx * 8, HALO + gx * 8 + 8)
             for part in range(2):
                 zs = slice(part * LANES, (part + 1) * LANES)
-                piece = recv_ref[src, part].reshape(8, 8, LANES)
-                field_ref[0, HALO + gx * 8 : HALO + gx * 8 + 8, ys, zs] = piece
-                pot_ref[xs, ys, zs] = recv_ref[src, 2 + part].reshape(8, 8, LANES)
-
-    def wrap(slot):
-        field_ref[slot, 0:HALO] = field_ref[slot, 32 : 32 + HALO]
-        field_ref[slot, 32 + HALO : 32 + 2 * HALO] = field_ref[slot, HALO : 2 * HALO]
-
-    def apply_group(slot, g):
-        x0 = HALO + g * 8
-        center = field_ref[slot, pl.ds(x0, 8)]
-        flat = center.reshape(256, 256)
-        high = flat.astype(jnp.bfloat16)
-        low = (flat - high.astype(jnp.float32)).astype(jnp.bfloat16)
-        dot = functools.partial(jnp.dot, preferred_element_type=jnp.float32)
-        shifts = dot(high, mat_ref[0]) + dot(low, mat_ref[0]) + dot(high, mat_ref[1])
-        shifts = shifts + (dot(mat_ref[2], high) + dot(mat_ref[2], low) + dot(mat_ref[3], high))
-        shifts = shifts.reshape(8, 32, 256)
-        total = (3.0 * STENCIL_WEIGHTS[0] * KINETIC) * center + (
-            STENCIL_WEIGHTS[1] * KINETIC
-        ) * shifts
-        for reach in range(1, 7):
-            pair = field_ref[slot, pl.ds(x0 + reach, 8)] + field_ref[slot, pl.ds(x0 - reach, 8)]
-            total = total + (STENCIL_WEIGHTS[reach] * KINETIC) * pair
-        total = total + pot_ref[pl.ds(g * 8, 8)] * center
-        return total, center
-
-    for step in range(DEGREE):
-        slot, other = step % 2, (step + 1) % 2
-        wrap(slot)
-
-        def advance(g, carry, step=step, slot=slot, other=other):
-            applied, center = apply_group(slot, g)
-            rows = pl.ds(HALO + g * 8, 8)
-            if step == 0:
-                following = (applied - FILTER_CENTER * center) * (1.0 / FILTER_HALFWIDTH)
-            else:
-                following = (applied - FILTER_CENTER * center) * (
-                    2.0 / FILTER_HALFWIDTH
-                ) - field_ref[other, rows]
-            field_ref[other, rows] = following
-            return carry
-
-        lax.fori_loop(0, 4, advance, 0)
-
-    slot = DEGREE % 2
-    wrap(slot)
+                tile = jnp.where(core == part, mine, theirs).reshape(8, 8, LANES)
+                local = (tile + (3.0 * STENCIL_WEIGHTS[0] * KINETIC - FILTER_CENTER)) * STEP
+                pot_ref[xs, ys, zs] = local
+                start = recv_ref[src, part].reshape(8, 8, LANES)
+                even_ref[rows, ys, zs] = start
+                odd_ref[rows, ys, zs] = 0.5 * (first_ref[xs, ys, zs] + local * start)
+
+    def apply_group(field_ref, g):
+        total, center = kinetic_group(field_ref, mats, g)
+        return total + pot_ref[g * 8 : g * 8 + 8] * center, center
+
+    for step in range(1, DEGREE):
+        current, previous = (odd_ref, even_ref) if step % 2 else (even_ref, odd_ref)
+        wrap(current)
+        for g in range(4):
+            total, _ = apply_group(current, g)
+            rows = slice(HALO + g * 8, HALO + g * 8 + 8)
+            previous[rows] = total - previous[rows]
+
+    last = odd_ref if DEGREE % 2 else even_ref
+    wrap(last)
     own = (lax.broadcasted_iota(jnp.int32, (8, 4, 8, LANES), 3) < 64) == (half == 0)
-
-    def finish(g, carry):
-        applied, center = apply_group(slot, g)
+    for g in range(4):
+        total, center = apply_group(last, g)
+        applied = total * (1.0 / STEP) + FILTER_CENTER * center
         tiles = center.reshape(8, 4, 8, 256)
         applied_tiles = applied.reshape(8, 4, 8, 256)
         moved = pltpu.roll(applied_tiles[..., LANES:].reshape(256, LANES), 64, 1)
-        gram_ref[:, g, :, 0:8] = tiles[..., :LANES]
-        gram_ref[:, g, :, 8:16] = applied_tiles[..., :LANES]
-        gram_ref[:, g, :, 16:24] = jnp.where(
+        out_ref[:, g, :, 0:8] = tiles[..., :LANES]
+        out_ref[:, g, :, 8:16] = applied_tiles[..., :LANES]
+        out_ref[:, g, :, 16:24] = jnp.where(
             own, tiles[..., LANES:], moved.reshape(8, 4, 8, LANES)
         )
-        return carry
-
-    lax.fori_loop(0, 4, finish, 0)
 
 
 def gram_kernel(recv_ref, out_ref):
@@ -224,21 +260,43 @@
     return lax.all_to_all(array, axes, split_axis=0, concat_axis=0, tiled=True)
 
 
+def pack(orbitals, potential):
+    hbm = pl.BlockSpec(memory_space=pltpu.HBM)
+    return pl.pallas_call(
+        pack_kernel,
+        out_shape=pltpu.HBM((2, 8, 3, 64, LANES), jnp.float32),
+        in_specs=[hbm, hbm],
+        out_specs=hbm,
+        scratch_shapes=[
+            pltpu.VMEM((8, 8, 8, 384), jnp.float32),
+            pltpu.VMEM((8, 8, 384), jnp.float32),
+            pltpu.VMEM((2, 8, 3, 64, LANES), jnp.float32),
+            pltpu.SemaphoreType.DMA((9,)),
+            pltpu.SemaphoreType.DMA((8,)),
+        ],
+        compiler_params=PARAMS,
+    )(*(pltpu.with_memory_space_constraint(a, pltpu.HBM) for a in (orbitals, potential)))
+
+
 def per_device(orbitals, potential):
-    packed = call(pack_kernel, (16, 4, 64, LANES), orbitals, potential)
+    packed = pack(orbitals, potential).reshape(16, 3, 64, LANES)
     windows = exchange(packed, GRID_AXES)
-    half = (lax.axis_index("gx") // 2).astype(jnp.int32).reshape(1)
-    matrices = jnp.asarray(band_matrices())
+    other = lax.ppermute(windows[:, 2], "gx", [(0, 1), (1, 0), (2, 3), (3, 2)])
+    place = lax.axis_index("gx")
+    place = jnp.stack([place // 2, place % 2]).astype(jnp.int32)
+    matrices = [jnp.asarray(m) for m in band_matrices()]
+    padded = pltpu.VMEM((32 + 2 * HALO, 32, 256), jnp.float32)
+    whole = pltpu.VMEM((32, 32, 256), jnp.float32)
+    first = call(kinetic_kernel, (32, 32, 256), windows, *matrices, scratch=(padded,))
     rows = call(
         filter_kernel,
         (8, 4, 4, 24, LANES),
-        half,
+        place,
         windows,
-        matrices,
-        scratch=(
-            pltpu.VMEM((2, 32 + 2 * HALO, 32, 256), jnp.float32),
-            pltpu.VMEM((32, 32, 256), jnp.float32),
-        ),
+        other,
+        first,
+        *matrices,
+        scratch=(padded, padded, whole),
         smem=1,
     )
     cells = exchange(rows.reshape(128, 24, LANES), ALL_AXES)

time: 116 us -> 105 us (0.905)
  blocking collectives: 47.5 us -> 77.4 us
  waiting for transfers between devices: 35.5 us -> 6.48 us
  starting transfers between devices: 13.6 us -> 6.18 us
  local copies, waits for them, and re-layouts: 3.36 us -> 0.06 us
  Pallas kernels: 15 us -> 13.3 us
    all_to_all x2 -> x3, blocking collectives: 47.5 us -> 77.4 us  [exchange(): return lax.all_to_all(array, axes, split_axis=0, concat_axis=0, tiled=True)]
    all_to_all x2 -> x1, waiting for transfers between devices: 35.5 us -> 6.43 us  [exchange(): return lax.all_to_all(array, axes, split_axis=0, concat_axis=0, tiled=True)]
    all_to_all x2 -> x1, starting transfers between devices: 13.6 us -> 4.38 us  [exchange(): return lax.all_to_all(array, axes, split_axis=0, concat_axis=0, tiled=True)]
    pallas_call x6, Pallas kernels: 15 us -> 11.1 us  [call(): pl.pallas_call(kernel, out_shape=outs[0] if single else outs, in_specs=sp...]
    unnamed x8 -> x6, local copies, waits for them, and re-layouts: 3.36 us -> 0.02 us
    pallas_call x0 -> x1, Pallas kernels: none -> 2.26 us  [pack(): pl.pallas_call(pack_kernel, out_shape=pltpu.HBM((2, 8, 3, 64, LANES), jnp...]
    ppermute x0 -> x1, starting transfers between devices: none -> 1.8 us  [per_device(): other = lax.ppermute(windows[:, 2], 'gx', [(0, 1), (1, 0), (2, 3), (3, 2)])]
  transfers between devices with their start and end apart: 2 -> 2, of which waited for: 2 -> 1; matrix products, arithmetic and copies ran while one was open for 0% -> 0% of each run, Pallas kernels for 1% -> 2%
where the time goes in v3:
time: 105 us; the launch traced here: 104 us
  blocking collectives  77.4 us (74%)
  Pallas kernels  13.3 us (13%)
  waiting for transfers between devices  6.48 us (6%)
  starting transfers between devices  6.18 us (6%)
    all_to_all x3, blocking collectives, exchange(): return lax.all_to_all(array, axes, split_axis=0, concat_axis=0, tiled=True)  77.4 us
    pallas_call x6, Pallas kernels, call(): pl.pallas_call(kernel, out_shape=outs[0] if single else outs, in_specs=sp...  11.1 us
    all_to_all x1, waiting for transfers between devices, exchange(): return lax.all_to_all(array, axes, split_axis=0, concat_axis=0, tiled=True)  6.43 us
    all_to_all x1, starting transfers between devices, exchange(): return lax.all_to_all(array, axes, split_axis=0, concat_axis=0, tiled=True)  4.38 us
    pallas_call x1, Pallas kernels, pack(): pl.pallas_call(pack_kernel, out_shape=pltpu.HBM((2, 8, 3, 64, LANES), jnp...  2.26 us
  transfers between devices with their start and end apart: 2, of which 1 were waited for; matrix products, arithmetic and copies ran while one was open for 0% of the time, Pallas kernels for 2%

profile of v3, /device:TPU:1, one launch (start us, length us, event | category | flops | bytes accessed | tf_op | source)
XLA Modules:
  0.0 104.2 jit_solution(1746817488198510948)
XLA Ops:
  0.6 2.3 %shard_map.76 = f32[2,8,3,64,128]{4,3,2,1,0:T(8,128)} custom-call(f32[8,8,8,384]{3,2,1,0:T(8,128)} %orb_ref.1, f32[8,8,384]{2,1,0:T(8,128)} %pot_ref.1), custom_call_target="tpu_custom_call" | custom-call | tf_op jit(solution)/shard_map/pallas_call | solution.py:265
  2.9 0.0 copy-start
  2.9 0.0 copy-start.1
  2.9 0.0 copy-start.2
  2.9 31.2 %all_to_all.20.recv_ref = f32[16,3,64,128]{3,2,1,0:T(8,128)S(1)} all-to-all(f32[16,3,64,128]{3,2,1,0:T(8,128)} %bitcast.11), channel_id=1, replica_groups=mesh['gx'=4,'gy'=4,'band'=8] {'gx','gy'}, dimensions={0} | all-to-all | bytes 3145728 | tf_op jit(solution)/shard_map/all_to_all | solution.py:260
  34.2 1.8 %collective-permute-start = (f32[16,64,128]{2,1,0:T(8,128)S(1)}, f32[16,64,128]{2,1,0:T(8,128)S(1)}, u32[]{:S(2)}, u32[]{:S(2)}) collective-permute-start(f32[16,64,128]{2,1,0:T(8,128)S(1)} %slice_bitcast_fusion), channel_id=1, source_target_pairs={{0,32},{32,0},{64,96},{96,64},{1,33},{33,1},{65,97},{97,65},{2,34}... | collective-permute-start | bytes 1572872 | tf_op jit(solution)/shard_map/ppermute | solution.py:284
  36.0 0.1 pad_add_fusion.place_ref
  36.0 0.0 copy-done
  36.0 0.0 copy-done.1
  36.1 0.0 copy-done.2
  36.1 1.4 %shard_map.77.first_ref = f32[32,32,256]{2,1,0:T(8,128)S(1)} custom-call(f32[16,3,64,128]{3,2,1,0:T(8,128)S(1)} %all_to_all.20.recv_ref, bf16[768,256]{1,0:T(8,128)(2,1)S(1)} %copy-done, bf16[128,256]{1,0:T(8,128)(2,1)S(1)} %copy-done.2, bf16[256,256]{1,0:T(8,128)(2,1)S(1)} %copy-done.1), custom_call_target="tpu_custom_call" | custom-call | tf_op jit(solution)/shard_map/pallas_call | solution.py:248
  37.5 0.0 collective-permute-done.other_ref
  37.5 6.7 %shard_map.78 = f32[8,4,4,24,128]{4,3,2,1,0:T(8,128)S(1)} custom-call(s32[2]{0:T(128)S(1)} %pad_add_fusion.place_ref, f32[16,3,64,128]{3,2,1,0:T(8,128)S(1)} %all_to_all.20.recv_ref, f32[16,64,128]{2,1,0:T(8,128)S(1)} %collective-permute-done.other_ref, f32[32,32,256]{2,1,0:T(8,128)S(1)} %shard_map.77.first_ref, bf16[768,256]{1,0:T(8,128)(2,1)S(1)} %copy-done, ...), custom_call_target="tpu_custom_call" | custom-call | tf_op jit(solution)/shard_map/pallas_call | solution.py:248
  44.2 29.3 %all_to_all.21 = f32[128,24,128]{2,1,0:T(8,128)S(1)} all-to-all(f32[128,24,128]{2,1,0:T(8,128)S(1)} %bitcast.10), channel_id=1, replica_groups=mesh['gx'=4,'gy'=4,'band'=8] {'band','gx','gy'}, dimensions={0} | all-to-all | bytes 3145728 | tf_op jit(solution)/shard_map/all_to_all | solution.py:260
  73.5 0.7 shard_map.79
  74.2 16.9 %all_to_all.22.recv_ref = f32[8,200,128]{2,1,0:T(8,128)S(1)} all-to-all(f32[8,200,128]{2,1,0:T(8,128)S(1)} %shard_map.79), channel_id=1, replica_groups=mesh['gx'=4,'gy'=4,'band'=8] {'band'}, dimensions={0} | all-to-all | bytes 1638400 | tf_op jit(solution)/shard_map/all_to_all | solution.py:260
  91.1 0.6 shard_map.81
  91.8 4.4 %all-to-all-start.3 = ((f32[16,8,128]{2,1,0:T(8,128)}), f32[16,8,128]{2,1,0:T(8,128)S(1)}, u32[]{:S(2)}, u32[]{:S(2)}) async-start(f32[16,8,128]{2,1,0:T(8,128)} %shard_map.81), calls=%async_computation.3 | async-start | bytes 131072 | tf_op jit(solution)/shard_map/all_to_all | solution.py:260
  96.2 0.9 shard_map.80
  97.1 6.4 %all-to-all-done.3.recv_ref = f32[16,8,128]{2,1,0:T(8,128)S(1)} async-done(((f32[16,8,128]{2,1,0:T(8,128)}), f32[16,8,128]{2,1,0:T(8,128)S(1)}, u32[]{:S(2)}, u32[]{:S(2)}) %all-to-all-start.3) | async-done | bytes 65568 | tf_op jit(solution)/shard_map/all_to_all | solution.py:260
  103.5 0.7 shard_map.82
  (1 shorter events, 0.0 us)
Async XLA Ops:
  2.9 33.2 %copy-start = (bf16[768,256]{1,0:T(8,128)(2,1)S(1)}, bf16[768,256]{1,0:T(8,128)(2,1)}, u32[]{:S(2)}) copy-start(bf16[768,256]{1,0:T(8,128)(2,1)} %constant.36.clone.z_ref) | copy-start | bytes 1179652
  2.9 33.1 %copy-start.1 = (bf16[256,256]{1,0:T(8,128)(2,1)S(1)}, bf16[256,256]{1,0:T(8,128)(2,1)}, u32[]{:S(2)}) copy-start(bf16[256,256]{1,0:T(8,128)(2,1)} %constant.38.clone.y_low_ref) | copy-start | bytes 393220
  2.9 33.1 %copy-start.2 = (bf16[128,256]{1,0:T(8,128)(2,1)S(1)}, bf16[128,256]{1,0:T(8,128)(2,1)}, u32[]{:S(2)}) copy-start(bf16[128,256]{1,0:T(8,128)(2,1)} %constant.37.clone.y_ref) | copy-start | bytes 196612
  34.2 3.3 %collective-permute-start = (f32[16,64,128]{2,1,0:T(8,128)S(1)}, f32[16,64,128]{2,1,0:T(8,128)S(1)}, u32[]{:S(2)}, u32[]{:S(2)}) collective-permute-start(f32[16,64,128]{2,1,0:T(8,128)S(1)} %slice_bitcast_fusion), channel_id=1, source_target_pairs={{0,32},{32,0},{64,96},{96,64},{1,33},{33,1},{65,97},{97,65},{2,34}... | collective-permute-start | bytes 1572872 | tf_op jit(solution)/shard_map/ppermute | solution.py:284
  91.8 11.7 %all-to-all-start.3 = ((f32[16,8,128]{2,1,0:T(8,128)}), f32[16,8,128]{2,1,0:T(8,128)S(1)}, u32[]{:S(2)}, u32[]{:S(2)}) async-start(f32[16,8,128]{2,1,0:T(8,128)} %shard_map.81), calls=%async_computation.3 | async-start | bytes 131072 | tf_op jit(solution)/shard_map/all_to_all | solution.py:260

commit v4 on v3

--- a/solution.py
+++ b/solution.py
@@ -25,21 +25,22 @@
 FILTER_HALFWIDTH = 20.0
 KINETIC = -0.5 / (GRID_SPACING * GRID_SPACING)
 STEP = 2.0 / FILTER_HALFWIDTH
+FIRST = STENCIL_WEIGHTS[1] * KINETIC * STEP
 GRID_AXES = ("gx", "gy")
 ALL_AXES = ("band", "gx", "gy")
 LANES = 128
-HALO = 8
 VMEM = pl.BlockSpec(memory_space=pltpu.VMEM)
-PARAMS = pltpu.CompilerParams(vmem_limit_bytes=48 * 1024 * 1024)
+PARAMS = pltpu.CompilerParams(vmem_limit_bytes=24 * 1024 * 1024)
 
 
 def lane_index(rows):
     return lax.broadcasted_iota(jnp.int32, (rows, LANES), 1)
 
 
-def pack_kernel(orb_ref, pot_ref, out_ref, orb, pot, packed, in_sems, out_sems):
-    loads = [pltpu.make_async_copy(pot_ref, pot, in_sems.at[8])]
-    loads += [pltpu.make_async_copy(orb_ref.at[j], orb.at[j], in_sems.at[j]) for j in range(8)]
+def pack_kernel(orb_ref, pot_ref, mats_ref, out_ref, mats_out_ref, orb, pot, sems):
+    loads = [pltpu.make_async_copy(pot_ref, pot, sems.at[8])]
+    loads += [pltpu.make_async_copy(orb_ref.at[j], orb.at[j], sems.at[j]) for j in range(8)]
+    loads += [pltpu.make_async_copy(mats_ref, mats_out_ref, sems.at[9])]
     for load in loads:
         load.start()
     lane = lane_index(64)
@@ -55,20 +56,14 @@
     pot_windows = windows(pot[...])
     for half in range(2):
         for j in range(8):
-            packed[half, j, 2] = pot_windows[half][j // 4]
-    stores = []
+            out_ref[half, j, 2] = pot_windows[half][j // 4]
     for j in range(8):
         loads[1 + j].wait()
         orb_windows = windows(orb[j])
         for half in range(2):
             for part in range(2):
-                packed[half, j, part] = orb_windows[half][part]
-        stores.append(
-            pltpu.make_async_copy(packed.at[:, j], out_ref.at[:, j], out_sems.at[j])
-        )
-        stores[-1].start()
-    for store in stores:
-        store.wait()
+                out_ref[half, j, part] = orb_windows[half][part]
+    loads[9].wait()
 
 
 def band_matrices():
@@ -88,91 +83,115 @@
 
     z_high, z_low = split(circulant(256))
     y_high, y_low = split(np.kron(np.eye(8), circulant(32)))
-    return np.concatenate([z_high, z_high, z_low]), np.concatenate(
-        [y_high[:128, :128], y_high[:128, :128]], axis=1
-    ), y_low
-
-
-def kinetic_group(field_ref, mats, g):
-    z_ref, y_ref, y_low_ref = mats
-    x0 = HALO + g * 8
-    center = field_ref[x0 : x0 + 8]
-    flat = center.reshape(256, 256)
-    high = flat.astype(jnp.bfloat16)
-    low = (flat - high.astype(jnp.float32)).astype(jnp.bfloat16)
-    dot = functools.partial(jnp.dot, preferred_element_type=jnp.float32)
-    shifts = dot(jnp.concatenate([high, low, high], axis=1), z_ref[...])
+    x_high, x_low = split(np.kron(circulant(32), np.eye(8)))
+    both = np.concatenate([y_high[:128, :128], y_high[:128, :128]], axis=1)
+    return np.concatenate([z_high, z_low, x_high, x_low, y_low, both])
+
+
+Z_HIGH, Z_LOW, X_HIGH, X_LOW, Y_LOW = (slice(i * 256, i * 256 + 256) for i in range(5))
+Y_BOTH = slice(5 * 256, 5 * 256 + 128)
+
+
+def dot(left, right):
+    return jnp.dot(left, right, preferred_element_type=jnp.float32)
+
+
+def split(field):
+    high = field.astype(jnp.bfloat16)
+    return high, (field - high.astype(jnp.float32)).astype(jnp.bfloat16)
+
+
+def add_along_x(field_ref, mats, out_ref, start):
+    for tile in range(4):
+        ys = slice(tile * 8, tile * 8 + 8)
+        if tile < 2:
+            field = field_ref[:, ys, :]
+            high, low = split(field.reshape(256, 256))
+            shifts = dot(mats[X_HIGH], high) + dot(mats[X_HIGH], low) + dot(mats[X_LOW], high)
+            out_ref[:, ys, :] = start(field, (slice(None), ys, slice(None))) + FIRST * shifts.reshape(
+                32, 8, 256
+            )
+            continue
+        for part in range(2):
+            zs = slice(part * LANES, (part + 1) * LANES)
+            planes = [field_ref[x, ys, zs] for x in range(32)]
+            for x in range(32):
+                total = start(planes[x], (x, ys, zs))
+                for reach in range(1, 7):
+                    pair = planes[(x + reach) % 32] + planes[(x - reach) % 32]
+                    total = total + (STENCIL_WEIGHTS[reach] * KINETIC * STEP) * pair
+                out_ref[x, ys, zs] = total
+
+
+def along_yz(field_ref, mats, g):
+    center = field_ref[g * 8 : g * 8 + 8]
+    high, low = split(center.reshape(256, 256))
+    shifts = dot(high, mats[Z_HIGH]) + dot(low, mats[Z_HIGH]) + dot(high, mats[Z_LOW])
     along_y = [
-        dot(y_ref[...], jnp.concatenate([high[rows], low[rows]], axis=0))
+        dot(mats[Y_BOTH], jnp.concatenate([high[rows], low[rows]], axis=0))
         for rows in (slice(0, 128), slice(128, 256))
     ]
-    shifts = shifts + jnp.concatenate(along_y, axis=0) + dot(y_low_ref[...], high)
-    total = (STENCIL_WEIGHTS[1] * KINETIC * STEP) * shifts.reshape(8, 32, 256)
-    for reach in range(1, 7):
-        pair = field_ref[x0 + reach : x0 + reach + 8] + field_ref[x0 - reach : x0 - reach + 8]
-        total = total + (STENCIL_WEIGHTS[reach] * KINETIC * STEP) * pair
-    return total, center
-
-
-def wrap(field_ref):
-    field_ref[0:HALO] = field_ref[32 : 32 + HALO]
-    field_ref[32 + HALO : 32 + 2 * HALO] = field_ref[HALO : 2 * HALO]
+    shifts = shifts + jnp.concatenate(along_y, axis=0) + dot(mats[Y_LOW], high)
+    return FIRST * shifts.reshape(8, 32, 256), center
 
 
 def domain(gx, gy):
     return gx * 4 + gy, slice(gx * 8, gx * 8 + 8), slice(gy * 8, gy * 8 + 8)
 
 
-def kinetic_kernel(recv_ref, z_ref, y_ref, y_low_ref, out_ref, field_ref):
+def own_tile_kernel(recv_ref, out_ref):
+    out_ref[...] = recv_ref[:, 2]
+
+
+def kinetic_kernel(recv_ref, mats, out_ref, field_ref):
     for gx in range(4):
         for gy in range(4):
             src, xs, ys = domain(gx, gy)
             for part in range(2):
-                piece = recv_ref[src, part].reshape(8, 8, LANES)
                 zs = slice(part * LANES, (part + 1) * LANES)
-                field_ref[HALO + gx * 8 : HALO + gx * 8 + 8, ys, zs] = piece
-    wrap(field_ref)
+                field_ref[xs, ys, zs] = recv_ref[src, part].reshape(8, 8, LANES)
+    add_along_x(field_ref, mats, out_ref, lambda field, at: 0.0)
     for g in range(4):
-        out_ref[g * 8 : g * 8 + 8], _ = kinetic_group(field_ref, (z_ref, y_ref, y_low_ref), g)
+        rows = slice(g * 8, g * 8 + 8)
+        out_ref[rows] = out_ref[rows] + along_yz(field_ref, mats, g)[0]
 
 
 def filter_kernel(
-    place_ref, recv_ref, other_ref, first_ref, z_ref, y_ref, y_low_ref, out_ref, even_ref, odd_ref, pot_ref
+    place_ref, recv_ref, other_ref, first_ref, mats, out_ref, even_ref, odd_ref, pot_ref
 ):
     half, core = place_ref[0], place_ref[1]
-    mats = (z_ref, y_ref, y_low_ref)
     for gx in range(4):
         for gy in range(4):
             src, xs, ys = domain(gx, gy)
             mine = recv_ref[src, 2]
             theirs = other_ref[src]
-            rows = slice(HALO + gx * 8, HALO + gx * 8 + 8)
             for part in range(2):
                 zs = slice(part * LANES, (part + 1) * LANES)
                 tile = jnp.where(core == part, mine, theirs).reshape(8, 8, LANES)
                 local = (tile + (3.0 * STENCIL_WEIGHTS[0] * KINETIC - FILTER_CENTER)) * STEP
                 pot_ref[xs, ys, zs] = local
                 start = recv_ref[src, part].reshape(8, 8, LANES)
-                even_ref[rows, ys, zs] = start
-                odd_ref[rows, ys, zs] = 0.5 * (first_ref[xs, ys, zs] + local * start)
-
-    def apply_group(field_ref, g):
-        total, center = kinetic_group(field_ref, mats, g)
-        return total + pot_ref[g * 8 : g * 8 + 8] * center, center
+                even_ref[xs, ys, zs] = start
+                odd_ref[xs, ys, zs] = 0.5 * (first_ref[xs, ys, zs] + local * start)
 
     for step in range(1, DEGREE):
         current, previous = (odd_ref, even_ref) if step % 2 else (even_ref, odd_ref)
-        wrap(current)
+        add_along_x(
+            current,
+            mats,
+            previous,
+            lambda field, at, previous=previous: pot_ref[at] * field - previous[at],
+        )
         for g in range(4):
-            total, _ = apply_group(current, g)
-            rows = slice(HALO + g * 8, HALO + g * 8 + 8)
-            previous[rows] = total - previous[rows]
-
-    last = odd_ref if DEGREE % 2 else even_ref
-    wrap(last)
+            rows = slice(g * 8, g * 8 + 8)
+            previous[rows] = previous[rows] + along_yz(current, mats, g)[0]
+
+    last, spare = (odd_ref, even_ref) if DEGREE % 2 else (even_ref, odd_ref)
+    add_along_x(last, mats, spare, lambda field, at: pot_ref[at] * field)
     own = (lax.broadcasted_iota(jnp.int32, (8, 4, 8, LANES), 3) < 64) == (half == 0)
     for g in range(4):
-        total, center = apply_group(last, g)
+        shifts, center = along_yz(last, mats, g)
+        total = spare[g * 8 : g * 8 + 8] + shifts
         applied = total * (1.0 / STEP) + FILTER_CENTER * center
         tiles = center.reshape(8, 4, 8, 256)
         applied_tiles = applied.reshape(8, 4, 8, 256)
@@ -262,32 +281,40 @@
 
 def pack(orbitals, potential):
     hbm = pl.BlockSpec(memory_space=pltpu.HBM)
+    matrices = jnp.asarray(band_matrices())
+    args = (orbitals, potential, matrices)
     return pl.pallas_call(
         pack_kernel,
-        out_shape=pltpu.HBM((2, 8, 3, 64, LANES), jnp.float32),
-        in_specs=[hbm, hbm],
-        out_specs=hbm,
+        out_shape=[
+            pltpu.VMEM((2, 8, 3, 64, LANES), jnp.float32),
+            pltpu.VMEM(matrices.shape, jnp.bfloat16),
+        ],
+        in_specs=[hbm] * 3,
+        out_specs=[VMEM] * 2,
         scratch_shapes=[
             pltpu.VMEM((8, 8, 8, 384), jnp.float32),
             pltpu.VMEM((8, 8, 384), jnp.float32),
-            pltpu.VMEM((2, 8, 3, 64, LANES), jnp.float32),
-            pltpu.SemaphoreType.DMA((9,)),
-            pltpu.SemaphoreType.DMA((8,)),
+            pltpu.SemaphoreType.DMA((10,)),
         ],
         compiler_params=PARAMS,
-    )(*(pltpu.with_memory_space_constraint(a, pltpu.HBM) for a in (orbitals, potential)))
+    )(*(pltpu.with_memory_space_constraint(a, pltpu.HBM) for a in args))
 
 
 def per_device(orbitals, potential):
-    packed = pack(orbitals, potential).reshape(16, 3, 64, LANES)
-    windows = exchange(packed, GRID_AXES)
-    other = lax.ppermute(windows[:, 2], "gx", [(0, 1), (1, 0), (2, 3), (3, 2)])
+    packed, matrices = pack(orbitals, potential)
+    windows = exchange(packed.reshape(16, 3, 64, LANES), GRID_AXES)
+    mine = pl.pallas_call(
+        own_tile_kernel,
+        out_shape=pltpu.VMEM((16, 64, LANES), jnp.float32),
+        in_specs=[VMEM],
+        out_specs=VMEM,
+        compiler_params=PARAMS,
+    )(windows)
+    other = lax.ppermute(mine, "gx", [(0, 1), (1, 0), (2, 3), (3, 2)])
     place = lax.axis_index("gx")
     place = jnp.stack([place // 2, place % 2]).astype(jnp.int32)
-    matrices = [jnp.asarray(m) for m in band_matrices()]
-    padded = pltpu.VMEM((32 + 2 * HALO, 32, 256), jnp.float32)
     whole = pltpu.VMEM((32, 32, 256), jnp.float32)
-    first = call(kinetic_kernel, (32, 32, 256), windows, *matrices, scratch=(padded,))
+    first = call(kinetic_kernel, (32, 32, 256), windows, matrices, scratch=(whole,))
     rows = call(
         filter_kernel,
         (8, 4, 4, 24, LANES),
@@ -295,8 +322,8 @@
         windows,
         other,
         first,
-        *matrices,
-        scratch=(padded, padded, whole),
+        matrices,
+        scratch=(whole, whole, whole),
         smem=1,
     )
     cells = exchange(rows.reshape(128, 24, LANES), ALL_AXES)

time: 105 us -> 103 us (0.981)
  Pallas kernels: 13.3 us -> 11.6 us
    pallas_call x1 -> x2, Pallas kernels: 2.26 us -> 1.62 us  [the longest x1 1.59 us: pack(): pl.pallas_call(pack_kernel, out_shape=[pltpu.VMEM((2, 8, 3, 64, LANES), j...]
  transfers between devices with their start and end apart: 2 -> 2, of which waited for: 1 -> 2; matrix products, arithmetic and copies ran while one was open for 0% -> 0% of each run, Pallas kernels for 2% -> 2%
where the time goes in v4:
time: 103 us; the launch traced here: 102 us
  blocking collectives  77.1 us (75%)
  Pallas kernels  11.6 us (11%)
  waiting for transfers between devices  6.72 us (7%)
  starting transfers between devices  6.18 us (6%)
    all_to_all x3, blocking collectives, exchange(): return lax.all_to_all(array, axes, split_axis=0, concat_axis=0, tiled=True)  77.1 us
    pallas_call x6, Pallas kernels, call(): pl.pallas_call(kernel, out_shape=outs[0] if single else outs, in_specs=sp...  10 us
    all_to_all x1, waiting for transfers between devices, exchange(): return lax.all_to_all(array, axes, split_axis=0, concat_axis=0, tiled=True)  6.43 us
    all_to_all x1, starting transfers between devices, exchange(): return lax.all_to_all(array, axes, split_axis=0, concat_axis=0, tiled=True)  4.38 us
  transfers between devices with their start and end apart: 2, of which 2 were waited for; matrix products, arithmetic and copies ran while one was open for 0% of the time, Pallas kernels for 2%

profile of v4, /device:TPU:1, one launch (start us, length us, event | category | flops | bytes accessed | tf_op | source)
XLA Modules:
  0.0 102.3 jit_solution(9830148674839132106)
XLA Ops:
  0.6 1.6 %shard_map.58 = (f32[2,8,3,64,128]{4,3,2,1,0:T(8,128)S(1)}, bf16[1408,256]{1,0:T(8,128)(2,1)S(1)}) custom-call(f32[8,8,8,384]{3,2,1,0:T(8,128)} %orb_ref.1, f32[8,8,384]{2,1,0:T(8,128)} %pot_ref.1, bf16[1408,256]{1,0:T(8,128)(2,1)} %constant.32.clone.mats_ref), custom_call_target="tpu_custom_call" | custom-call | tf_op jit(solution)/shard_map/pallas_call | solution.py:286
  2.2 30.8 %all_to_all.20.recv_ref = f32[16,3,64,128]{3,2,1,0:T(8,128)S(1)} all-to-all(f32[16,3,64,128]{3,2,1,0:T(8,128)S(1)} %bitcast.7), channel_id=1, replica_groups=mesh['gx'=4,'gy'=4,'band'=8] {'gx','gy'}, dimensions={0} | all-to-all | bytes 3145728 | tf_op jit(solution)/shard_map/all_to_all | solution.py:279
  33.1 1.8 %collective-permute-start = (f32[16,64,128]{2,1,0:T(8,128)S(1)}, f32[16,64,128]{2,1,0:T(8,128)S(1)}, u32[]{:S(2)}, u32[]{:S(2)}) collective-permute-start(f32[16,64,128]{2,1,0:T(8,128)S(1)} %shard_map.59), channel_id=1, source_target_pairs={{0,32},{32,0},{64,96},{96,64},{1,33},{33,1},{65,97},{97,65},{2,34}... | collective-permute-start | bytes 1572872 | tf_op jit(solution)/shard_map/ppermute | solution.py:313
  34.9 0.1 pad_add_fusion.place_ref
  35.0 1.2 %shard_map.60.first_ref = f32[32,32,256]{2,1,0:T(8,128)S(1)} custom-call(f32[16,3,64,128]{3,2,1,0:T(8,128)S(1)} %all_to_all.20.recv_ref, bf16[1408,256]{1,0:T(8,128)(2,1)S(1)} %get-tuple-element.8.mats), custom_call_target="tpu_custom_call" | custom-call | tf_op jit(solution)/shard_map/pallas_call | solution.py:267
  36.2 0.3 collective-permute-done.other_ref
  36.4 5.9 %shard_map.61 = f32[8,4,4,24,128]{4,3,2,1,0:T(8,128)S(1)} custom-call(s32[2]{0:T(128)S(1)} %pad_add_fusion.place_ref, f32[16,3,64,128]{3,2,1,0:T(8,128)S(1)} %all_to_all.20.recv_ref, f32[16,64,128]{2,1,0:T(8,128)S(1)} %collective-permute-done.other_ref, f32[32,32,256]{2,1,0:T(8,128)S(1)} %shard_map.60.first_ref, bf16[1408,256]{1,0:T(8,128)(2,1)S(1)} %get-tuple-element.8.mats), custom_call_target="tpu_custom_call" | custom-call | tf_op jit(solution)/shard_map/pallas_call | solution.py:267
  42.4 29.3 %all_to_all.21 = f32[128,24,128]{2,1,0:T(8,128)S(1)} all-to-all(f32[128,24,128]{2,1,0:T(8,128)S(1)} %bitcast.6), channel_id=1, replica_groups=mesh['gx'=4,'gy'=4,'band'=8] {'band','gx','gy'}, dimensions={0} | all-to-all | bytes 3145728 | tf_op jit(solution)/shard_map/all_to_all | solution.py:279
  71.7 0.7 shard_map.62
  72.4 16.9 %all_to_all.22.recv_ref = f32[8,200,128]{2,1,0:T(8,128)S(1)} all-to-all(f32[8,200,128]{2,1,0:T(8,128)S(1)} %shard_map.62), channel_id=1, replica_groups=mesh['gx'=4,'gy'=4,'band'=8] {'band'}, dimensions={0} | all-to-all | bytes 1638400 | tf_op jit(solution)/shard_map/all_to_all | solution.py:279
  89.3 0.6 shard_map.64
  89.9 4.4 %all-to-all-start.3 = ((f32[16,8,128]{2,1,0:T(8,128)}), f32[16,8,128]{2,1,0:T(8,128)S(1)}, u32[]{:S(2)}, u32[]{:S(2)}) async-start(f32[16,8,128]{2,1,0:T(8,128)} %shard_map.64), calls=%async_computation.3 | async-start | bytes 131072 | tf_op jit(solution)/shard_map/all_to_all | solution.py:279
  94.3 0.9 shard_map.63
  95.2 6.4 %all-to-all-done.3.recv_ref = f32[16,8,128]{2,1,0:T(8,128)S(1)} async-done(((f32[16,8,128]{2,1,0:T(8,128)}), f32[16,8,128]{2,1,0:T(8,128)S(1)}, u32[]{:S(2)}, u32[]{:S(2)}) %all-to-all-start.3) | async-done | bytes 65568 | tf_op jit(solution)/shard_map/all_to_all | solution.py:279
  101.7 0.7 shard_map.65
  (1 shorter events, 0.0 us)
Async XLA Ops:
  33.1 3.3 %collective-permute-start = (f32[16,64,128]{2,1,0:T(8,128)S(1)}, f32[16,64,128]{2,1,0:T(8,128)S(1)}, u32[]{:S(2)}, u32[]{:S(2)}) collective-permute-start(f32[16,64,128]{2,1,0:T(8,128)S(1)} %shard_map.59), channel_id=1, source_target_pairs={{0,32},{32,0},{64,96},{96,64},{1,33},{33,1},{65,97},{97,65},{2,34}... | collective-permute-start | bytes 1572872 | tf_op jit(solution)/shard_map/ppermute | solution.py:313
  89.9 11.7 %all-to-all-start.3 = ((f32[16,8,128]{2,1,0:T(8,128)}), f32[16,8,128]{2,1,0:T(8,128)S(1)}, u32[]{:S(2)}, u32[]{:S(2)}) async-start(f32[16,8,128]{2,1,0:T(8,128)} %shard_map.64), calls=%async_computation.3 | async-start | bytes 131072 | tf_op jit(solution)/shard_map/all_to_all | solution.py:279

commit v5 on v4

--- a/solution.py
+++ b/solution.py
@@ -143,7 +143,7 @@
     out_ref[...] = recv_ref[:, 2]
 
 
-def kinetic_kernel(recv_ref, mats, out_ref, field_ref):
+def kinetic_kernel(recv_ref, mats, field_ref, out_ref):
     for gx in range(4):
         for gy in range(4):
             src, xs, ys = domain(gx, gy)
@@ -153,11 +153,11 @@
     add_along_x(field_ref, mats, out_ref, lambda field, at: 0.0)
     for g in range(4):
         rows = slice(g * 8, g * 8 + 8)
-        out_ref[rows] = out_ref[rows] + along_yz(field_ref, mats, g)[0]
+        out_ref[rows] = 0.5 * (out_ref[rows] + along_yz(field_ref, mats, g)[0])
 
 
 def filter_kernel(
-    place_ref, recv_ref, other_ref, first_ref, mats, out_ref, even_ref, odd_ref, pot_ref
+    place_ref, recv_ref, other_ref, start_ref, first_ref, mats, out_ref, even_ref, odd_ref, pot_ref
 ):
     half, core = place_ref[0], place_ref[1]
     for gx in range(4):
@@ -170,21 +170,20 @@
                 tile = jnp.where(core == part, mine, theirs).reshape(8, 8, LANES)
                 local = (tile + (3.0 * STENCIL_WEIGHTS[0] * KINETIC - FILTER_CENTER)) * STEP
                 pot_ref[xs, ys, zs] = local
-                start = recv_ref[src, part].reshape(8, 8, LANES)
-                even_ref[xs, ys, zs] = start
-                odd_ref[xs, ys, zs] = 0.5 * (first_ref[xs, ys, zs] + local * start)
+                odd_ref[xs, ys, zs] = first_ref[xs, ys, zs] + 0.5 * local * start_ref[xs, ys, zs]
 
     for step in range(1, DEGREE):
-        current, previous = (odd_ref, even_ref) if step % 2 else (even_ref, odd_ref)
+        current, following = (odd_ref, even_ref) if step % 2 else (even_ref, odd_ref)
+        previous = start_ref if step == 1 else following
         add_along_x(
             current,
             mats,
-            previous,
+            following,
             lambda field, at, previous=previous: pot_ref[at] * field - previous[at],
         )
         for g in range(4):
             rows = slice(g * 8, g * 8 + 8)
-            previous[rows] = previous[rows] + along_yz(current, mats, g)[0]
+            following[rows] = following[rows] + along_yz(current, mats, g)[0]
 
     last, spare = (odd_ref, even_ref) if DEGREE % 2 else (even_ref, odd_ref)
     add_along_x(last, mats, spare, lambda field, at: pot_ref[at] * field)
@@ -243,26 +242,37 @@
 
 
 def band_sum_kernel(recv_ref, out_ref):
-    total = jnp.sum(recv_ref[:, 192:200], axis=0)
+    total = jnp.sum(recv_ref[:, 24], axis=0)
     out_ref[...] = jnp.broadcast_to(total[None], (16, 8, LANES))
 
 
-def unpack_kernel(recv_ref, out_ref):
-    for x in range(8):
-        for part in range(3):
-            piece = recv_ref[x, part * 64 : part * 64 + 64].reshape(8, 8, LANES)
-            out_ref[:, x, :, part * LANES : (part + 1) * LANES] = piece
-
-
-def sum_kernel(recv_ref, margin_ref, hamiltonian_ref, *, scale):
-    total = jnp.sum(recv_ref[...], axis=0) * scale
-    margin_ref[...] = total[:, :64]
-    hamiltonian_ref[...] = pltpu.roll(total, 64, 1)[:, :64]
-
-
-def call(kernel, shapes, *args, scratch=(), smem=0):
+def last_kernel(home_ref, sums_ref, out_ref, margin_ref, hamiltonian_ref, whole, rows, sems, *, scale):
+    copies = []
+
+    def send(source, target):
+        copies.append(pltpu.make_async_copy(source, target, sems.at[len(copies)]))
+        copies[-1].start()
+
+    for j in range(8):
+        for x in range(8):
+            for part in range(3):
+                zs = slice(part * LANES, (part + 1) * LANES)
+                whole[j, x, :, zs] = home_ref[x, part * 8 + j]
+        send(whole.at[j], out_ref.at[j])
+        if j == 0:
+            total = jnp.sum(sums_ref[...], axis=0) * scale
+            rows[0] = total[:, :64]
+            rows[1] = pltpu.roll(total, 64, 1)[:, :64]
+            send(rows.at[0], margin_ref)
+            send(rows.at[1], hamiltonian_ref)
+    for copy in copies:
+        copy.wait()
+
+
+def call(kernel, shapes, *args, scratch=(), smem=0, keep=False):
     single = not isinstance(shapes, list)
-    outs = [jax.ShapeDtypeStruct(s, jnp.float32) for s in ([shapes] if single else shapes)]
+    place = pltpu.VMEM if keep else jax.ShapeDtypeStruct
+    outs = [place(s, jnp.float32) for s in ([shapes] if single else shapes)]
     specs = [pl.BlockSpec(memory_space=pltpu.SMEM)] * smem + [VMEM] * (len(args) - smem)
     result = pl.pallas_call(
         kernel,
@@ -280,7 +290,6 @@
 
 
 def pack(orbitals, potential):
-    hbm = pl.BlockSpec(memory_space=pltpu.HBM)
     matrices = jnp.asarray(band_matrices())
     args = (orbitals, potential, matrices)
     return pl.pallas_call(
@@ -289,7 +298,7 @@
             pltpu.VMEM((2, 8, 3, 64, LANES), jnp.float32),
             pltpu.VMEM(matrices.shape, jnp.bfloat16),
         ],
-        in_specs=[hbm] * 3,
+        in_specs=[pl.BlockSpec(memory_space=pltpu.HBM)] * 3,
         out_specs=[VMEM] * 2,
         scratch_shapes=[
             pltpu.VMEM((8, 8, 8, 384), jnp.float32),
@@ -303,24 +312,21 @@
 def per_device(orbitals, potential):
     packed, matrices = pack(orbitals, potential)
     windows = exchange(packed.reshape(16, 3, 64, LANES), GRID_AXES)
-    mine = pl.pallas_call(
-        own_tile_kernel,
-        out_shape=pltpu.VMEM((16, 64, LANES), jnp.float32),
-        in_specs=[VMEM],
-        out_specs=VMEM,
-        compiler_params=PARAMS,
-    )(windows)
+    mine = call(own_tile_kernel, (16, 64, LANES), windows, keep=True)
     other = lax.ppermute(mine, "gx", [(0, 1), (1, 0), (2, 3), (3, 2)])
     place = lax.axis_index("gx")
     place = jnp.stack([place // 2, place % 2]).astype(jnp.int32)
     whole = pltpu.VMEM((32, 32, 256), jnp.float32)
-    first = call(kinetic_kernel, (32, 32, 256), windows, matrices, scratch=(whole,))
+    start, first = call(
+        kinetic_kernel, [(32, 32, 256), (32, 32, 256)], windows, matrices, keep=True
+    )
     rows = call(
         filter_kernel,
         (8, 4, 4, 24, LANES),
         place,
         windows,
         other,
+        start,
         first,
         matrices,
         scratch=(whole, whole, whole),
@@ -328,14 +334,24 @@
     )
     cells = exchange(rows.reshape(128, 24, LANES), ALL_AXES)
     outgoing = call(gram_kernel, (8, 200, LANES), cells.reshape(128 * 24, LANES))
-    home = exchange(outgoing, "band")
-    sums = exchange(call(band_sum_kernel, (16, 8, LANES), home), GRID_AXES)
-    filtered = call(unpack_kernel, (8, 8, 8, 384), home)
-    scale = 1.0 / (8 * 8 * 384)
-    margin, hamiltonian = call(
-        functools.partial(sum_kernel, scale=scale), [(8, 64), (8, 64)], sums
-    )
-    return filtered, margin, hamiltonian
+    home = exchange(outgoing, "band").reshape(8, 25, 8, LANES)
+    sums = exchange(call(band_sum_kernel, (16, 8, LANES), home, keep=True), GRID_AXES)
+    return pl.pallas_call(
+        functools.partial(last_kernel, scale=1.0 / (8 * 8 * 384)),
+        out_shape=[
+            pltpu.HBM((8, 8, 8, 384), jnp.float32),
+            pltpu.HBM((8, 64), jnp.float32),
+            pltpu.HBM((8, 64), jnp.float32),
+        ],
+        in_specs=[VMEM] * 2,
+        out_specs=[pl.BlockSpec(memory_space=pltpu.HBM)] * 3,
+        scratch_shapes=[
+            pltpu.VMEM((8, 8, 8, 384), jnp.float32),
+            pltpu.VMEM((2, 8, 64), jnp.float32),
+            pltpu.SemaphoreType.DMA((10,)),
+        ],
+        compiler_params=PARAMS,
+    )(home, sums)
 
 
 def solution(mesh):

time: 103 us -> 102 us (level)
  blocking collectives: 77.1 us -> 88.5 us
  waiting for transfers between devices: 6.72 us -> 0.2 us
  starting transfers between devices: 6.18 us -> 1.8 us
  Pallas kernels: 11.6 us -> 10.2 us
    all_to_all x3 -> x4, blocking collectives: 77.1 us -> 88.5 us  [exchange(): return lax.all_to_all(array, axes, split_axis=0, concat_axis=0, tiled=True)]
    all_to_all x1 -> x0, waiting for transfers between devices: 6.43 us -> none  [exchange(): return lax.all_to_all(array, axes, split_axis=0, concat_axis=0, tiled=True)]
    all_to_all x1 -> x0, starting transfers between devices: 4.38 us -> none  [exchange(): return lax.all_to_all(array, axes, split_axis=0, concat_axis=0, tiled=True)]
    pallas_call x6 -> x5, Pallas kernels: 10 us -> 7.64 us  [call(): pl.pallas_call(kernel, out_shape=outs[0] if single else outs, in_specs=sp...]
  transfers between devices with their start and end apart: 2 -> 1, of which waited for: 2 -> 1; matrix products, arithmetic and copies ran while one was open for 0% -> 0% of each run, Pallas kernels for 2% -> 1%
where the time goes in v5:
time: 102 us; the launch traced here: 101 us
  blocking collectives  88.5 us (87%)
  Pallas kernels  10.2 us (10%)
  starting transfers between devices  1.8 us (2%)
    all_to_all x4, blocking collectives, exchange(): return lax.all_to_all(array, axes, split_axis=0, concat_axis=0, tiled=True)  88.5 us
    pallas_call x5, Pallas kernels, call(): pl.pallas_call(kernel, out_shape=outs[0] if single else outs, in_specs=sp...  7.64 us
  transfers between devices with their start and end apart: 1, of which 1 were waited for; matrix products, arithmetic and copies ran while one was open for 0% of the time, Pallas kernels for 1%

profile of v5, /device:TPU:1, one launch (start us, length us, event | category | flops | bytes accessed | tf_op | source)
XLA Modules:
  0.0 101.5 jit_solution(3399560441188047680)
XLA Ops:
  0.6 1.6 %shard_map.58 = (f32[2,8,3,64,128]{4,3,2,1,0:T(8,128)S(1)}, bf16[1408,256]{1,0:T(8,128)(2,1)S(1)}) custom-call(f32[8,8,8,384]{3,2,1,0:T(8,128)} %orb_ref.1, f32[8,8,384]{2,1,0:T(8,128)} %pot_ref.1, bf16[1408,256]{1,0:T(8,128)(2,1)} %constant.32.clone.mats_ref), custom_call_target="tpu_custom_call" | custom-call | tf_op jit(solution)/shard_map/pallas_call | solution.py:295
  2.2 30.8 %all_to_all.20.recv_ref = f32[16,3,64,128]{3,2,1,0:T(8,128)S(1)} all-to-all(f32[16,3,64,128]{3,2,1,0:T(8,128)S(1)} %bitcast.10), channel_id=1, replica_groups=mesh['gx'=4,'gy'=4,'band'=8] {'gx','gy'}, dimensions={0} | all-to-all | bytes 3145728 | tf_op jit(solution)/shard_map/all_to_all | solution.py:289
  33.1 1.8 %collective-permute-start = (f32[16,64,128]{2,1,0:T(8,128)S(1)}, f32[16,64,128]{2,1,0:T(8,128)S(1)}, u32[]{:S(2)}, u32[]{:S(2)}) collective-permute-start(f32[16,64,128]{2,1,0:T(8,128)S(1)} %shard_map.59), channel_id=1, source_target_pairs={{0,32},{32,0},{64,96},{96,64},{1,33},{33,1},{65,97},{97,65},{2,34}... | collective-permute-start | bytes 1572872 | tf_op jit(solution)/shard_map/ppermute | solution.py:316
  34.9 0.1 pad_add_fusion.place_ref
  35.0 1.3 %shard_map.60 = (f32[32,32,256]{2,1,0:T(8,128)S(1)}, f32[32,32,256]{2,1,0:T(8,128)S(1)}) custom-call(f32[16,3,64,128]{3,2,1,0:T(8,128)S(1)} %all_to_all.20.recv_ref, bf16[1408,256]{1,0:T(8,128)(2,1)S(1)} %get-tuple-element.8.mats), custom_call_target="tpu_custom_call" | custom-call | tf_op jit(solution)/shard_map/pallas_call | solution.py:277
  36.2 0.2 collective-permute-done.other_ref
  36.4 5.6 %shard_map.61 = f32[8,4,4,24,128]{4,3,2,1,0:T(8,128)S(1)} custom-call(s32[2]{0:T(128)S(1)} %pad_add_fusion.place_ref, f32[16,3,64,128]{3,2,1,0:T(8,128)S(1)} %all_to_all.20.recv_ref, f32[16,64,128]{2,1,0:T(8,128)S(1)} %collective-permute-done.other_ref, f32[32,32,256]{2,1,0:T(8,128)S(1)} %get-tuple-element.9.start_ref, ...), custom_call_target="tpu_custom_call" | custom-call | tf_op jit(solution)/shard_map/pallas_call | solution.py:277
  42.1 29.3 %all_to_all.21 = f32[128,24,128]{2,1,0:T(8,128)S(1)} all-to-all(f32[128,24,128]{2,1,0:T(8,128)S(1)} %bitcast.9), channel_id=1, replica_groups=mesh['gx'=4,'gy'=4,'band'=8] {'band','gx','gy'}, dimensions={0} | all-to-all | bytes 3145728 | tf_op jit(solution)/shard_map/all_to_all | solution.py:289
  71.4 0.7 shard_map.62
  72.1 16.9 %all_to_all.22 = f32[8,200,128]{2,1,0:T(8,128)S(1)} all-to-all(f32[8,200,128]{2,1,0:T(8,128)S(1)} %shard_map.62), channel_id=1, replica_groups=mesh['gx'=4,'gy'=4,'band'=8] {'band'}, dimensions={0} | all-to-all | bytes 1638400 | tf_op jit(solution)/shard_map/all_to_all | solution.py:289
  89.0 11.5 %all_to_all.23.sums_ref = f32[16,8,128]{2,1,0:T(8,128)S(1)} all-to-all(f32[16,8,128]{2,1,0:T(8,128)S(1)} %shard_map.63), channel_id=1, replica_groups=mesh['gx'=4,'gy'=4,'band'=8] {'gx','gy'}, dimensions={0} | all-to-all | bytes 131072 | tf_op jit(solution)/shard_map/all_to_all | solution.py:289
  100.5 1.0 shard_map.64
  (2 shorter events, 0.0 us)
Async XLA Ops:
  33.1 3.3 %collective-permute-start = (f32[16,64,128]{2,1,0:T(8,128)S(1)}, f32[16,64,128]{2,1,0:T(8,128)S(1)}, u32[]{:S(2)}, u32[]{:S(2)}) collective-permute-start(f32[16,64,128]{2,1,0:T(8,128)S(1)} %shard_map.59), channel_id=1, source_target_pairs={{0,32},{32,0},{64,96},{96,64},{1,33},{33,1},{65,97},{97,65},{2,34}... | collective-permute-start | bytes 1572872 | tf_op jit(solution)/shard_map/ppermute | solution.py:316

commit v6 on v5

--- a/solution.py
+++ b/solution.py
@@ -157,9 +157,10 @@
 
 
 def filter_kernel(
-    place_ref, recv_ref, other_ref, start_ref, first_ref, mats, out_ref, even_ref, odd_ref, pot_ref
+    recv_ref, other_ref, start_ref, first_ref, mats, out_ref, even_ref, odd_ref, pot_ref
 ):
-    half, core = place_ref[0], place_ref[1]
+    place = lax.axis_index("gx")
+    half, core = place // 2, place % 2
     for gx in range(4):
         for gy in range(4):
             src, xs, ys = domain(gx, gy)
@@ -269,11 +270,11 @@
         copy.wait()
 
 
-def call(kernel, shapes, *args, scratch=(), smem=0, keep=False):
+def call(kernel, shapes, *args, scratch=(), keep=False):
     single = not isinstance(shapes, list)
     place = pltpu.VMEM if keep else jax.ShapeDtypeStruct
     outs = [place(s, jnp.float32) for s in ([shapes] if single else shapes)]
-    specs = [pl.BlockSpec(memory_space=pltpu.SMEM)] * smem + [VMEM] * (len(args) - smem)
+    specs = [VMEM] * len(args)
     result = pl.pallas_call(
         kernel,
         out_shape=outs[0] if single else outs,
@@ -314,8 +315,6 @@
     windows = exchange(packed.reshape(16, 3, 64, LANES), GRID_AXES)
     mine = call(own_tile_kernel, (16, 64, LANES), windows, keep=True)
     other = lax.ppermute(mine, "gx", [(0, 1), (1, 0), (2, 3), (3, 2)])
-    place = lax.axis_index("gx")
-    place = jnp.stack([place // 2, place % 2]).astype(jnp.int32)
     whole = pltpu.VMEM((32, 32, 256), jnp.float32)
     start, first = call(
         kinetic_kernel, [(32, 32, 256), (32, 32, 256)], windows, matrices, keep=True
@@ -323,14 +322,12 @@
     rows = call(
         filter_kernel,
         (8, 4, 4, 24, LANES),
-        place,
         windows,
         other,
         start,
         first,
         matrices,
         scratch=(whole, whole, whole),
-        smem=1,
     )
     cells = exchange(rows.reshape(128, 24, LANES), ALL_AXES)
     outgoing = call(gram_kernel, (8, 200, LANES), cells.reshape(128 * 24, LANES))

time: 102 us -> 101 us (level)
  no operation moved by 1% of the time
where the time goes in v6:
time: 101 us
  blocking collectives  88.5 us (88%)
  Pallas kernels  9.63 us (10%)
  starting transfers between devices  1.8 us (2%)
    all_to_all x4, blocking collectives, exchange(): return lax.all_to_all(array, axes, split_axis=0, concat_axis=0, tiled=True)  88.5 us
    pallas_call x5, Pallas kernels, call(): pl.pallas_call(kernel, out_shape=outs[0] if single else outs, in_specs=sp...  7.03 us
  transfers between devices with their start and end apart: 1, of which 1 were waited for; matrix products, arithmetic and copies ran while one was open for 0% of the time, Pallas kernels for 1%

profile of v6, /device:TPU:1, one launch (start us, length us, event | category | flops | bytes accessed | tf_op | source)
XLA Modules:
  0.0 100.9 jit_solution(15744505593421145802)
XLA Ops:
  0.6 1.6 %shard_map.58 = (f32[2,8,3,64,128]{4,3,2,1,0:T(8,128)S(1)}, bf16[1408,256]{1,0:T(8,128)(2,1)S(1)}) custom-call(f32[8,8,8,384]{3,2,1,0:T(8,128)} %orb_ref.1, f32[8,8,384]{2,1,0:T(8,128)} %pot_ref.1, bf16[1408,256]{1,0:T(8,128)(2,1)} %constant.2.clone.mats_ref), custom_call_target="tpu_custom_call" | custom-call | tf_op jit(solution)/shard_map/pallas_call | solution.py:296
  2.2 30.8 %all_to_all.20.recv_ref = f32[16,3,64,128]{3,2,1,0:T(8,128)S(1)} all-to-all(f32[16,3,64,128]{3,2,1,0:T(8,128)S(1)} %bitcast.8), channel_id=1, replica_groups=mesh['gx'=4,'gy'=4,'band'=8] {'gx','gy'}, dimensions={0} | all-to-all | bytes 3145728 | tf_op jit(solution)/shard_map/all_to_all | solution.py:290
  33.1 1.8 %collective-permute-start = (f32[16,64,128]{2,1,0:T(8,128)S(1)}, f32[16,64,128]{2,1,0:T(8,128)S(1)}, u32[]{:S(2)}, u32[]{:S(2)}) collective-permute-start(f32[16,64,128]{2,1,0:T(8,128)S(1)} %shard_map.59), channel_id=1, source_target_pairs={{0,32},{32,0},{64,96},{96,64},{1,33},{33,1},{65,97},{97,65},{2,34}... | collective-permute-start | bytes 1572872 | tf_op jit(solution)/shard_map/ppermute | solution.py:317
  34.9 1.3 %shard_map.60 = (f32[32,32,256]{2,1,0:T(8,128)S(1)}, f32[32,32,256]{2,1,0:T(8,128)S(1)}) custom-call(f32[16,3,64,128]{3,2,1,0:T(8,128)S(1)} %all_to_all.20.recv_ref, bf16[1408,256]{1,0:T(8,128)(2,1)S(1)} %get-tuple-element.8.mats), custom_call_target="tpu_custom_call" | custom-call | tf_op jit(solution)/shard_map/pallas_call | solution.py:278
  36.2 0.3 collective-permute-done.other_ref
  36.4 5.0 %shard_map.61 = f32[8,4,4,24,128]{4,3,2,1,0:T(8,128)S(1)} custom-call(f32[16,3,64,128]{3,2,1,0:T(8,128)S(1)} %all_to_all.20.recv_ref, f32[16,64,128]{2,1,0:T(8,128)S(1)} %collective-permute-done.other_ref, f32[32,32,256]{2,1,0:T(8,128)S(1)} %get-tuple-element.9.start_ref, f32[32,32,256]{2,1,0:T(8,128)S(1)} %get-tuple-element.10.first_ref, ...), custom_call_target="tpu_custom_call" | custom-call | tf_op jit(solution)/shard_map/pallas_call | solution.py:278
  41.5 29.3 %all_to_all.21 = f32[128,24,128]{2,1,0:T(8,128)S(1)} all-to-all(f32[128,24,128]{2,1,0:T(8,128)S(1)} %bitcast.7), channel_id=1, replica_groups=mesh['gx'=4,'gy'=4,'band'=8] {'band','gx','gy'}, dimensions={0} | all-to-all | bytes 3145728 | tf_op jit(solution)/shard_map/all_to_all | solution.py:290
  70.8 0.7 shard_map.62
  71.5 16.9 %all_to_all.22 = f32[8,200,128]{2,1,0:T(8,128)S(1)} all-to-all(f32[8,200,128]{2,1,0:T(8,128)S(1)} %shard_map.62), channel_id=1, replica_groups=mesh['gx'=4,'gy'=4,'band'=8] {'band'}, dimensions={0} | all-to-all | bytes 1638400 | tf_op jit(solution)/shard_map/all_to_all | solution.py:290
  88.4 11.4 %all_to_all.23.sums_ref = f32[16,8,128]{2,1,0:T(8,128)S(1)} all-to-all(f32[16,8,128]{2,1,0:T(8,128)S(1)} %shard_map.63), channel_id=1, replica_groups=mesh['gx'=4,'gy'=4,'band'=8] {'gx','gy'}, dimensions={0} | all-to-all | bytes 131072 | tf_op jit(solution)/shard_map/all_to_all | solution.py:290
  99.9 1.0 %shard_map.64 = (f32[8,8,8,384]{3,2,1,0:T(8,128)}, f32[8,64]{1,0:T(8,128)}, f32[8,64]{1,0:T(8,128)}) custom-call(f32[8,25,8,128]{3,2,1,0:T(8,128)S(1)} %bitcast.5, f32[16,8,128]{2,1,0:T(8,128)S(1)} %all_to_all.23.sums_ref), custom_call_target="tpu_custom_call" | custom-call | tf_op jit(solution)/shard_map/pallas_call | solution.py:336
  (2 shorter events, 0.0 us)
Async XLA Ops:
  33.1 3.3 %collective-permute-start = (f32[16,64,128]{2,1,0:T(8,128)S(1)}, f32[16,64,128]{2,1,0:T(8,128)S(1)}, u32[]{:S(2)}, u32[]{:S(2)}) collective-permute-start(f32[16,64,128]{2,1,0:T(8,128)S(1)} %shard_map.59), channel_id=1, source_target_pairs={{0,32},{32,0},{64,96},{96,64},{1,33},{33,1},{65,97},{97,65},{2,34}... | collective-permute-start | bytes 1572872 | tf_op jit(solution)/shard_map/ppermute | solution.py:317

commit v7 on v6

--- a/solution.py
+++ b/solution.py
@@ -41,7 +41,7 @@
     loads = [pltpu.make_async_copy(pot_ref, pot, sems.at[8])]
     loads += [pltpu.make_async_copy(orb_ref.at[j], orb.at[j], sems.at[j]) for j in range(8)]
     loads += [pltpu.make_async_copy(mats_ref, mats_out_ref, sems.at[9])]
-    for load in loads:
+    for load in loads[1:9] + [loads[0], loads[9]]:
         load.start()
     lane = lane_index(64)
 
@@ -52,17 +52,17 @@
             (z2, jnp.where(lane < 32, z0, z1)),
         )
 
-    loads[0].wait()
-    pot_windows = windows(pot[...])
-    for half in range(2):
-        for j in range(8):
-            out_ref[half, j, 2] = pot_windows[half][j // 4]
     for j in range(8):
         loads[1 + j].wait()
         orb_windows = windows(orb[j])
         for half in range(2):
             for part in range(2):
                 out_ref[half, j, part] = orb_windows[half][part]
+    loads[0].wait()
+    pot_windows = windows(pot[...])
+    for half in range(2):
+        for j in range(8):
+            out_ref[half, j, 2] = pot_windows[half][j // 4]
     loads[9].wait()
 
 

time: 101 us -> 101 us (level)
  no operation moved by 1% of the time
where the time goes in v7:
time: 101 us
  blocking collectives  88.5 us (88%)
  Pallas kernels  9.63 us (10%)
  starting transfers between devices  1.8 us (2%)
    all_to_all x4, blocking collectives, exchange(): return lax.all_to_all(array, axes, split_axis=0, concat_axis=0, tiled=True)  88.5 us
    pallas_call x5, Pallas kernels, call(): pl.pallas_call(kernel, out_shape=outs[0] if single else outs, in_specs=sp...  7.03 us
  transfers between devices with their start and end apart: 1, of which 1 were waited for; matrix products, arithmetic and copies ran while one was open for 0% of the time, Pallas kernels for 1%

profile of v7, /device:TPU:1, one launch (start us, length us, event | category | flops | bytes accessed | tf_op | source)
XLA Modules:
  0.0 100.9 jit_solution(3072479879161099890)
XLA Ops:
  0.6 1.6 %shard_map.58 = (f32[2,8,3,64,128]{4,3,2,1,0:T(8,128)S(1)}, bf16[1408,256]{1,0:T(8,128)(2,1)S(1)}) custom-call(f32[8,8,8,384]{3,2,1,0:T(8,128)} %orb_ref.1, f32[8,8,384]{2,1,0:T(8,128)} %pot_ref.1, bf16[1408,256]{1,0:T(8,128)(2,1)} %constant.2.clone.mats_ref), custom_call_target="tpu_custom_call" | custom-call | tf_op jit(solution)/shard_map/pallas_call | solution.py:296
  2.2 30.8 %all_to_all.20.recv_ref = f32[16,3,64,128]{3,2,1,0:T(8,128)S(1)} all-to-all(f32[16,3,64,128]{3,2,1,0:T(8,128)S(1)} %bitcast.8), channel_id=1, replica_groups=mesh['gx'=4,'gy'=4,'band'=8] {'gx','gy'}, dimensions={0} | all-to-all | bytes 3145728 | tf_op jit(solution)/shard_map/all_to_all | solution.py:290
  33.1 1.8 %collective-permute-start = (f32[16,64,128]{2,1,0:T(8,128)S(1)}, f32[16,64,128]{2,1,0:T(8,128)S(1)}, u32[]{:S(2)}, u32[]{:S(2)}) collective-permute-start(f32[16,64,128]{2,1,0:T(8,128)S(1)} %shard_map.59), channel_id=1, source_target_pairs={{0,32},{32,0},{64,96},{96,64},{1,33},{33,1},{65,97},{97,65},{2,34}... | collective-permute-start | bytes 1572872 | tf_op jit(solution)/shard_map/ppermute | solution.py:317
  34.9 1.3 %shard_map.60 = (f32[32,32,256]{2,1,0:T(8,128)S(1)}, f32[32,32,256]{2,1,0:T(8,128)S(1)}) custom-call(f32[16,3,64,128]{3,2,1,0:T(8,128)S(1)} %all_to_all.20.recv_ref, bf16[1408,256]{1,0:T(8,128)(2,1)S(1)} %get-tuple-element.8.mats), custom_call_target="tpu_custom_call" | custom-call | tf_op jit(solution)/shard_map/pallas_call | solution.py:278
  36.2 0.3 collective-permute-done.other_ref
  36.4 5.0 %shard_map.61 = f32[8,4,4,24,128]{4,3,2,1,0:T(8,128)S(1)} custom-call(f32[16,3,64,128]{3,2,1,0:T(8,128)S(1)} %all_to_all.20.recv_ref, f32[16,64,128]{2,1,0:T(8,128)S(1)} %collective-permute-done.other_ref, f32[32,32,256]{2,1,0:T(8,128)S(1)} %get-tuple-element.9.start_ref, f32[32,32,256]{2,1,0:T(8,128)S(1)} %get-tuple-element.10.first_ref, ...), custom_call_target="tpu_custom_call" | custom-call | tf_op jit(solution)/shard_map/pallas_call | solution.py:278
  41.5 29.3 %all_to_all.21 = f32[128,24,128]{2,1,0:T(8,128)S(1)} all-to-all(f32[128,24,128]{2,1,0:T(8,128)S(1)} %bitcast.7), channel_id=1, replica_groups=mesh['gx'=4,'gy'=4,'band'=8] {'band','gx','gy'}, dimensions={0} | all-to-all | bytes 3145728 | tf_op jit(solution)/shard_map/all_to_all | solution.py:290
  70.8 0.7 shard_map.62
  71.5 16.9 %all_to_all.22 = f32[8,200,128]{2,1,0:T(8,128)S(1)} all-to-all(f32[8,200,128]{2,1,0:T(8,128)S(1)} %shard_map.62), channel_id=1, replica_groups=mesh['gx'=4,'gy'=4,'band'=8] {'band'}, dimensions={0} | all-to-all | bytes 1638400 | tf_op jit(solution)/shard_map/all_to_all | solution.py:290
  88.4 11.4 %all_to_all.23.sums_ref = f32[16,8,128]{2,1,0:T(8,128)S(1)} all-to-all(f32[16,8,128]{2,1,0:T(8,128)S(1)} %shard_map.63), channel_id=1, replica_groups=mesh['gx'=4,'gy'=4,'band'=8] {'gx','gy'}, dimensions={0} | all-to-all | bytes 131072 | tf_op jit(solution)/shard_map/all_to_all | solution.py:290
  99.9 1.0 %shard_map.64 = (f32[8,8,8,384]{3,2,1,0:T(8,128)}, f32[8,64]{1,0:T(8,128)}, f32[8,64]{1,0:T(8,128)}) custom-call(f32[8,25,8,128]{3,2,1,0:T(8,128)S(1)} %bitcast.5, f32[16,8,128]{2,1,0:T(8,128)S(1)} %all_to_all.23.sums_ref), custom_call_target="tpu_custom_call" | custom-call | tf_op jit(solution)/shard_map/pallas_call | solution.py:336
  (2 shorter events, 0.0 us)
Async XLA Ops:
  33.1 3.3 %collective-permute-start = (f32[16,64,128]{2,1,0:T(8,128)S(1)}, f32[16,64,128]{2,1,0:T(8,128)S(1)}, u32[]{:S(2)}, u32[]{:S(2)}) collective-permute-start(f32[16,64,128]{2,1,0:T(8,128)S(1)} %shard_map.59), channel_id=1, source_target_pairs={{0,32},{32,0},{64,96},{96,64},{1,33},{33,1},{65,97},{97,65},{2,34}... | collective-permute-start | bytes 1572872 | tf_op jit(solution)/shard_map/ppermute | solution.py:317
